TPU v7x, 256 devices: a whole 4x4x8 slice. The times are simulated.
256 devices in a mesh: seq: 16 (over y, z_hi, core), tp: 16 (over x, z_lo).
Axes of the slice: x: 4, y: 4, z: 8 (z_hi: 2, z_lo: 4; z = z_hi * 4 + z_lo), core: 2. Of those that a mesh axis runs over, the one named last changes fastest.
Arguments:
- hidden_in: bfloat16 [512, 4608], P(('seq', 'tp')), may hold values from -3 to 3
- query: bfloat16 [512, 4096], P('seq', 'tp'), may hold values from -6 to 6
- kv_pool: bfloat16 [8192, 2, 16, 4, 128], P('seq', None, 'tp'), may hold values from -6 to 6
- kv_map: int32 [512, 16], P(None, 'seq'), may hold values from 0 to 511, as said below
- lengths: int32 [512], replicated, may hold values from 16 to 64
- o_weight: bfloat16 [4096, 4608], P('tp'), may hold values from -0.09375 to 0.09375
- norm_gain: float32 [4608], replicated, may hold values from 0.5 to 1.5
- width_class: int32 [4], replicated, may hold values from 0 to 3, as said below
- gate_weight: bfloat16 [4608, 36864], P(None, ('seq', 'tp')), may hold values from -0.09375 to 0.09375
- up_weight: bfloat16 [4608, 36864], P(None, ('seq', 'tp')), may hold values from -0.09375 to 0.09375
- down_weight: bfloat16 [36864, 4608], P(('seq', 'tp')), may hold values from -0.03125 to 0.03125
Outputs:
- hidden_out: bfloat16 [512, 4608], P(('seq', 'tp'))
Inputs may be any that keep to these rules, and one draw needn't show every extreme that they name: Each column of kv_map names every slot from 0 to 511 exactly once. `width_class`: groups g and g + k share a class only when k is a multiple of 4.
All inputs are finite; a program needn't handle non-finite values.
Results may differ from a plain program's by a relative error of at most 0.023.
Values may be sent and summed in bfloat16 or wider, within the bound.
A program may use at most 64 MiB of HBM per device.

v0:
```python
import jax
import jax.numpy as jnp
from jax import lax
from jax.sharding import PartitionSpec as P

FF = 36864
WIDTHS = 4
GROUP = 128
QPRE = 144


SOFTCAP = 50.0
EPS = 1e-06


def rms_normalize(residual, norm_gain):
    wide = residual.astype(jnp.float32)
    scale = lax.rsqrt(jnp.mean(wide * wide, axis=1, keepdims=True) + EPS)
    return (wide * scale * norm_gain[None, :]).astype(jnp.bfloat16)


def attend(query_rows, keys, values, row_lengths):
    count = query_rows.shape[0]
    local_heads = keys.shape[1]
    span = keys.shape[2]
    queries = query_rows.reshape(count, local_heads, -1, keys.shape[3])
    scores = jnp.einsum(
        "rkgd,rkpd->rkgp", queries, keys, preferred_element_type=jnp.float32
    ) * QPRE ** (-0.5)
    capped = SOFTCAP * jnp.tanh(scores / SOFTCAP)
    positions = jnp.arange(span, dtype=jnp.int32)
    live = positions[None, :] < row_lengths[:, None]
    weights = jnp.where(live[:, None, None, :], jnp.exp(capped), 0.0)
    totals = jnp.sum(weights, axis=3)
    numer = jnp.einsum(
        "rkgp,rkpd->rkgd", weights.astype(jnp.bfloat16), values, preferred_element_type=jnp.float32
    )
    return (numer, totals)


def feed_forward(normed_rows, width_class, gate_weight, up_weight, down_weight, unit_start):
    count = normed_rows.shape[0]
    gate = jnp.dot(normed_rows, gate_weight, preferred_element_type=jnp.float32)
    up = jnp.dot(normed_rows, up_weight, preferred_element_type=jnp.float32)
    row_ids = jnp.arange(count, dtype=jnp.int32)
    group_ids = jnp.arange(width_class.shape[0], dtype=jnp.int32)
    matches = row_ids[:, None] // GROUP == group_ids[None, :]
    row_class = jnp.sum(jnp.where(matches, width_class[None, :], 0), axis=1)
    limit = (row_class + 1) * (FF // WIDTHS)
    units = unit_start + jnp.arange(gate.shape[1], dtype=jnp.int32)
    active = units[None, :] < limit[:, None]
    hidden = jnp.where(active, jax.nn.gelu(gate, approximate=True) * up, 0.0).astype(jnp.bfloat16)
    return jnp.dot(hidden, down_weight, preferred_element_type=jnp.float32)


def body(
    hidden_in,
    query,
    kv_pool,
    kv_map,
    lengths,
    o_weight,
    norm_gain,
    width_class,
    gate_weight,
    up_weight,
    down_weight,
):
    seq_pos = lax.axis_index("seq")
    own_rows = query.shape[0]
    picked = kv_pool[kv_map[:, 0]]
    arranged = lax.all_to_all(picked[:, :, :, None], "seq", split_axis=0, concat_axis=3, tiled=True)
    arranged = arranged.reshape(own_rows, 2, picked.shape[2], -1, picked.shape[4])
    row_lengths = lax.dynamic_slice_in_dim(lengths, seq_pos * own_rows, own_rows, 0)
    numer, totals = attend(query, arranged[:, 0], arranged[:, 1], row_lengths)
    attended = (numer / totals[..., None]).reshape(numer.shape[0], -1).astype(jnp.bfloat16)
    unit_start = lax.axis_index(("seq", "tp")) * gate_weight.shape[1]
    projected = lax.psum_scatter(
        jnp.dot(attended, o_weight, preferred_element_type=jnp.float32).astype(jnp.bfloat16),
        "tp",
        scatter_dimension=0,
        tiled=True,
    ).astype(jnp.float32)
    residual = (hidden_in.astype(jnp.float32) + projected).astype(jnp.bfloat16)
    normed = rms_normalize(residual, norm_gain)
    terms = feed_forward(
        lax.all_gather(normed, ("seq", "tp"), axis=0, tiled=True),
        width_class,
        gate_weight,
        up_weight,
        down_weight,
        unit_start,
    )
    summed = lax.psum_scatter(terms, ("seq", "tp"), scatter_dimension=0, tiled=True)
    return (residual.astype(jnp.float32) + summed).astype(jnp.bfloat16)


def solution(mesh):
    placed = (
        P(("seq", "tp"), None),
        P("seq", "tp"),
        P("seq", None, "tp", None, None),
        P(None, "seq"),
        P(),
        P("tp", None),
        P(),
        P(),
        P(None, ("seq", "tp")),
        P(None, ("seq", "tp")),
        P(("seq", "tp"), None),
    )
    return jax.shard_map(
        body, mesh=mesh, in_specs=placed, out_specs=P(("seq", "tp"), None), check_vma=False
    )
```

profile of v0, /device:TPU:8, one launch (start us, length us, event | category | flops | bytes accessed | tf_op | source)
XLA Modules:
  0.0 1225.8 jit_solution(4960975162170080404)
XLA Ops:
  6.5 0.8 compare_select_fusion
  7.4 3.9 gather_fusion
  11.3 11.6 all-to-all-start
  22.9 0.0 all-reduce.5.cloned.1.call-start
  23.0 0.8 dynamic_slice.3
  23.7 0.1 iota_compare_fusion
  23.8 26.7 %all-to-all-done = bf16[512,2,1,1,4,128]{5,4,1,3,2,0:T(4,128)(2,1)S(1)} async-done(((bf16[512,2,1,1,4,128]{5,4,1,3,2,0:T(4,128)(2,1)}), bf16[512,2,1,1,4,128]{5,4,1,3,2,0:T(4,128)(2,1)S(1)}, u32[]{:S(2)}, u32[]{:S(2)}) %all-to-all-start) | async-done | bytes 1048608 | tf_op jit(solution)/shard_map/all_to_all | solution.py:72
  50.5 0.6 copy.14
  51.1 0.0 copy-start.5
  51.1 0.0 copy-start.2
  51.1 0.0 copy-start.1
  51.2 0.5 fusion.41
  51.6 0.3 fusion.8
  51.9 1.2 convolution_convert_fusion
  53.1 0.0 all-reduce.5.cloned.1.call-update
  53.2 0.0 all-gather.3.cloned.1.call-start
  53.2 0.6 dynamic-slice
  54.5 151.4 %all-reduce.5.cloned.1.call-done = bf16[32,4608]{1,0:T(8,128)(2,1)} async-done(((bf16[32,4608]{1,0:T(8,128)(2,1)}), bf16[32,4608]{1,0:T(8,128)(2,1)}) %all-reduce.5.cloned.1.call-update) | async-done | bytes 294928
  205.8 0.0 copy-done.2
  205.8 1.0 fusion.25
  206.9 0.7 fusion.29
  207.6 0.0 all-gather.3.cloned.1.call-update
  207.6 0.0 all-reduce.7.cloned.1.call-start
  207.7 0.0 copy-done.4
  207.7 0.1 select_reduce_fusion
  207.8 683.1 %all-gather.3.cloned.1.call-done = bf16[256,2,4608]{2,1,0:T(2,128)(2,1)} async-done(((bf16[1,2,4608]{2,1,0:T(2,128)(2,1)}), bf16[256,2,4608]{2,1,0:T(2,128)(2,1)}) %all-gather.3.cloned.1.call-update) | async-done | bytes 4718608 | tf_op jit(solution)/shard_map/all_gather | solution.py:87
  890.9 7.5 reshape.127
  898.4 4.4 fusion.42
  902.8 9.8 fusion.2
  912.7 0.0 all-reduce.7.cloned.1.call-update
  912.7 305.1 %all-reduce.7.cloned.1.call-done = f32[512,4608]{1,0:T(8,128)} async-done(((f32[512,4608]{1,0:T(8,128)}), f32[512,4608]{1,0:T(8,128)}) %all-reduce.7.cloned.1.call-update) | async-done | bytes 9437200
  1217.7 1.5 fusion.28
  (13 shorter events, 0.1 us)
Async XLA Ops:
  6.5 45.4 %copy-start = (bf16[256,4608]{1,0:T(8,128)(2,1)S(1)}, bf16[256,4608]{1,0:T(8,128)(2,1)}, u32[]{:S(2)}) copy-start(bf16[256,4608]{1,0:T(8,128)(2,1)} %param.16) | copy-start | bytes 7077892
  6.5 16.4 %copy-start.3 = (bf16[32,256]{1,0:T(8,128)(2,1)S(1)}, bf16[32,256]{1,0:T(8,128)(2,1)}, u32[]{:S(2)}) copy-start(bf16[32,256]{1,0:T(8,128)(2,1)} %param.12) | copy-start | bytes 49156
  11.3 39.2 %all-to-all-start = ((bf16[512,2,1,1,4,128]{5,4,1,3,2,0:T(4,128)(2,1)}), bf16[512,2,1,1,4,128]{5,4,1,3,2,0:T(4,128)(2,1)S(1)}, u32[]{:S(2)}, u32[]{:S(2)}) async-start(bf16[512,2,1,1,4,128]{5,4,1,3,2,0:T(4,128)(2,1)} %bitcast.2), calls=%async_computation | async-start | bytes 2097152 | tf_op jit(solution)/shard_map/all_to_all | solution.py:72
  22.9 182.9 %all-reduce.5.cloned.1.call-start = ((), (), s32[]{:S(2)}) async-start(), calls=%async_computation.2 | async-start | bytes 589824
  51.1 2.1 copy-start.5
  51.1 154.7 %copy-start.2 = (bf16[2,4608]{1,0:T(2,128)(2,1)S(1)}, bf16[2,4608]{1,0:T(2,128)(2,1)}, u32[]{:S(2)}) copy-start(bf16[2,4608]{1,0:T(2,128)(2,1)} %param.11) | copy-start | bytes 55300
  51.1 155.8 %copy-start.1 = (f32[4608]{0:T(1024)S(1)}, f32[4608]{0:T(1024)}, u32[]{:S(2)}) copy-start(f32[4608]{0:T(1024)} %param.17) | copy-start | bytes 55300
  51.6 156.1 %copy-start.4 = (s32[4]{0:T(128)S(1)}, s32[4]{0:T(128)}, u32[]{:S(2)}) copy-start(s32[4]{0:T(128)} %param.18) | copy-start | bytes 52
  53.2 837.8 %all-gather.3.cloned.1.call-start = ((), (), s32[]{:S(2)}) async-start(), calls=%async_computation.1 | async-start | bytes 4737024 | tf_op jit(solution)/shard_map/all_gather | solution.py:87
  207.6 1010.1 %all-reduce.7.cloned.1.call-start = ((), (), s32[]{:S(2)}) async-start(), calls=%async_computation.3 | async-start | bytes 18874368
Sparse Core Ops, SparseCore 0:
  53.3 152.5 all-reduce.4
  207.9 683.0 all-gather.2
  912.8 304.8 all-reduce.6
where the time goes:
time: 1230 us
  waiting for transfers between devices  1170 us (95%)
  matrix products  16.2 us (1%)
  between operations  13.9 us (1%)
  local copies, waits for them, and re-layouts  13.4 us (1%)
    all_gather x1, waiting for transfers between devices, body(): lax.all_gather(normed, ('seq', 'tp'), axis=0, tiled=True)  683 us
    unnamed x5, waiting for transfers between devices  456 us
    all_to_all x1, waiting for transfers between devices, body(): lax.all_to_all(picked[:, :, :, None], 'seq', split_axis=0, concat_axis=3,...  26.7 us
  transfers between devices with their start and end apart: 4, of which 4 were waited for; matrix products, arithmetic and copies ran while one was open for 0% of the time, Pallas kernels for 0%

commit v1 on v0

v1 whole, which is shorter than its diff:
```python
import functools

import jax
import jax.numpy as jnp
from jax import lax
from jax.experimental import pallas as pl
from jax.experimental.pallas import tpu as pltpu
from jax.sharding import PartitionSpec as P

D = 4608
FF = 36864
WIDTHS = 4
QPRE = 144
SOFTCAP = 50.0
EPS = 1e-06
QD = D // 4
UNITS = FF // 256
MESH = pl.DeviceIdType.MESH
F32 = jnp.float32
BF16 = jnp.bfloat16


def dev(x, y, z, c):
    return (y * 4 + (z // 4) * 2 + c, x * 4 + z % 4)


def dot_nt(a, b):
    return lax.dot_general(a, b, (((1,), (1,)), ((), ())), preferred_element_type=F32)


def remote(src, dst, ssem, rsem, target):
    return pltpu.make_async_remote_copy(
        src_ref=src, dst_ref=dst, send_sem=ssem, recv_sem=rsem, device_id=target, device_id_type=MESH
    )


def kernel(
    hid_ref, q_ref, kvm_ref, len_ref, wc_ref, gain_ref, kv_hbm, ow_hbm, wg_hbm, wu_hbm, wd_hbm,
    out_ref,
    kv_v, ow_v, wg_v, wu_v, wd_v,
    qb, oh, oht, qs, ls, ns, nb, nr, nrx, sb, rb, g, xs, accg, accu, hs, p, r, rx1, t, rx2, zb, rx3, res,
    lsem, a1s, a1r, a3s, a3r, bs, br, c1s, c1r, c2s, c2r, c3s, c3r, cfs, cfr,
    d0s, d0r, d1s, d1r, d2s, d2r, d3s, d3r,
):
    seq = lax.axis_index("seq")
    tp = lax.axis_index("tp")
    y, zh, c = seq // 4, (seq // 2) % 2, seq % 2
    x, zl = tp // 4, tp % 4
    z = zh * 4 + zl
    sib = dev(x, y, z, 1 - c)

    seq_offs = [(dy, dh) for dy in range(4) for dh in range(2) if (dy, dh) != (0, 0)]
    tp_offs = [(dx, dl) for dx in (2, 1, 3, 0) for dl in (2, 1, 3, 0) if (dx, dl) != (0, 0)]
    peers = [sib]
    peers += [dev(x, (y + dy) % 4, ((zh + dh) % 2) * 4 + zl, c) for dy, dh in seq_offs]
    peers += [dev((x + dx) % 4, y, zh * 4 + (zl + dl) % 4, c) for dx, dl in tp_offs]
    peers += [dev(x, y, (1 - zh) * 4 + (zl + dl) % 4, c) for dl in (1, 2, 3)]
    bar = pltpu.get_barrier_semaphore()
    for peer in peers:
        pl.semaphore_signal(bar, inc=1, device_id=peer, device_id_type=MESH)

    loads = [
        pltpu.make_async_copy(kv_hbm, kv_v, lsem.at[0]),
        pltpu.make_async_copy(ow_hbm, ow_v, lsem.at[1]),
        pltpu.make_async_copy(wg_hbm, wg_v, lsem.at[2]),
        pltpu.make_async_copy(wu_hbm, wu_v, lsem.at[3]),
        pltpu.make_async_copy(wd_hbm, wd_v, lsem.at[4]),
    ]
    for load in loads:
        load.start()
    pl.semaphore_wait(bar, len(peers))

    sends = []
    a1 = []
    for i, (dy, dh) in enumerate(seq_offs):
        to = dev(x, (y + dy) % 4, ((zh + dh) % 2) * 4 + zl, c)
        cp = remote(q_ref, qb.at[seq], a1s.at[i], a1r.at[i], to)
        cp.start()
        sends.append(cp)
    cp = remote(q_ref, qb.at[seq], a1s.at[7], a1r.at[7], sib)
    cp.start()
    sends.append(cp)
    qb[seq] = q_ref[...]

    row_id = lax.broadcasted_iota(jnp.int32, (512, 128), 0).astype(F32)
    lane_id = lax.broadcasted_iota(jnp.int32, (128, 128), 1).astype(F32)
    for j in range(4):
        kvrow = kvm_ref[pl.ds(j, 1), :].astype(F32)
        oh[:, pl.ds(j * 128, 128)] = jnp.where(row_id == kvrow, 1.0, 0.0).astype(BF16)
        kvcol = jnp.transpose(jnp.broadcast_to(kvrow, (128, 128)))
        for k in range(4):
            oht[pl.ds(j * 128, 128), pl.ds(k * 128, 128)] = jnp.where(
                kvcol == lane_id + float(k * 128), 1.0, 0.0
            ).astype(BF16)
        lrow = len_ref[pl.ds(j, 1), :].astype(F32)
        xs[pl.ds(j * 128, 128), pl.ds(0, 128)] = jnp.transpose(
            jnp.broadcast_to(lrow, (128, 128))
        ).astype(BF16)
    ls[...] = jnp.dot(oh[...], xs[:, pl.ds(0, 128)], preferred_element_type=F32)

    for i, (dy, dh) in enumerate(seq_offs):
        frm = ((y - dy) % 4) * 4 + ((zh + dh) % 2) * 2 + c
        a = remote(q_ref, qb.at[frm], a1s.at[i], a1r.at[i], sib)
        a.wait_recv()
        cp = remote(qb.at[frm], qb.at[frm], a1s.at[8 + i], a1r.at[8 + i], sib)
        cp.start()
        sends.append(cp)
    remote(q_ref, qb.at[seq], a1s.at[7], a1r.at[7], sib).wait_recv()
    for i, (dy, dh) in enumerate(seq_offs):
        frm = ((y - dy) % 4) * 4 + ((zh + dh) % 2) * 2 + (1 - c)
        remote(qb.at[frm], qb.at[frm], a1s.at[8 + i], a1r.at[8 + i], sib).wait_recv()

    qs[...] = jnp.dot(
        oh[...], qb[...].reshape(512, 256), preferred_element_type=F32
    ).astype(BF16)
    loads[0].wait()

    first = seq * 4
    a_id = lax.broadcasted_iota(jnp.int32, (64, 256), 0) & 31
    b_id = lax.broadcasted_iota(jnp.int32, (64, 256), 1)
    own = (a_id == (b_id >> 3)) & ((b_id & 4) == 0)
    pos = (first + (b_id & 3)).astype(F32)
    lane = lax.broadcasted_iota(jnp.int32, (32, 128), 1)

    def attend(blk, _):
        rows = pl.ds(pl.multiple_of(blk * 32, 32), 32)
        keys = kv_v[pl.ds(pl.multiple_of(blk * 256, 256), 256), :]
        qq = jnp.concatenate([qs[rows, pl.ds(0, 128)], qs[rows, pl.ds(128, 128)]], axis=0)
        s = dot_nt(qq, keys)
        e = jnp.exp(SOFTCAP * jnp.tanh(s * (QPRE ** (-0.5) / SOFTCAP)))
        lb = ls[rows, :]
        lb = jnp.concatenate([lb, lb], axis=0)
        lb = jnp.concatenate([lb, lb], axis=1)
        w = jnp.where(own & (pos < lb), e, 0.0)
        tot = jnp.sum(w, axis=1, keepdims=True)
        wv = pltpu.roll(w, 4, 1).astype(BF16)
        num = jnp.dot(wv, keys, preferred_element_type=F32)
        ns[rows, pl.ds(0, 128)] = num[:32].astype(BF16)
        ns[rows, pl.ds(128, 128)] = num[32:].astype(BF16)
        both = jnp.where((lane & 63) < 32, tot[:32], tot[32:])
        hi = both.astype(BF16).astype(F32)
        ns[rows, pl.ds(256, 128)] = jnp.where(lane < 64, hi, both - hi).astype(BF16)
        return 0

    lax.fori_loop(0, 16, attend, 0)

    for k in range(4):
        v = jnp.dot(
            oht[pl.ds(k * 128, 128), :], ns[...], preferred_element_type=F32
        ).astype(BF16)
        for h in range(2):
            for cc in range(2):
                at = (h * 2 + cc) * 32
                nb[cc, k * 2 + h] = v[at : at + 32]
    cp = remote(nb.at[1 - c], nr, a3s.at[7], a3r.at[7], sib)
    cp.start()
    sends.append(cp)
    cp.wait_recv()

    low_half = lax.broadcasted_iota(jnp.int32, (32, 128), 1) < 64

    def split_total(block):
        both = block + pltpu.roll(block, 64, 1)
        hi = both.astype(BF16).astype(F32)
        return both, jnp.where(low_half, hi, both - hi).astype(BF16)

    def pair_sum(k, _):
        v = nb[c, k].astype(F32) + nr[k].astype(F32)
        nb[c, k, :, pl.ds(0, 256)] = v[:, :256].astype(BF16)
        nb[c, k, :, pl.ds(256, 128)] = split_total(v[:, 256:])[1]
        return 0

    lax.fori_loop(0, 8, pair_sum, 0)
    a3 = []
    for i, (dy, dh) in enumerate(seq_offs):
        yt, ht = (y + dy) % 4, (zh + dh) % 2
        cp = remote(nb.at[c, yt * 2 + ht], nrx.at[i], a3s.at[i], a3r.at[i], dev(x, yt, ht * 4 + zl, c))
        cp.start()
        sends.append(cp)
        a3.append(cp)
    total = nb[c, y * 2 + zh].astype(F32)
    for i in range(7):
        a3[i].wait_recv()
        total = total + nrx[i].astype(F32)
    tot = split_total(total[:, 256:])[0]
    att = jnp.concatenate(
        [total[:, :128] / tot[:, 0:1], total[:, 128:256] / tot[:, 32:33]], axis=1
    ).astype(BF16)

    loads[1].wait()
    rid = lax.broadcasted_iota(jnp.int32, (32, QD), 0)
    row0 = x * 8 + zl * 2
    bcp = []
    for dx in (2, 1, 3, 0):
        xt = (x + dx) % 4
        cols = pl.ds(pl.multiple_of(xt * QD, 128), QD)
        v = jnp.dot(att, ow_v[:, cols], preferred_element_type=F32)
        hid = hid_ref[:, cols].astype(F32)
        v = v + jnp.where(rid == row0, hid[0:1], 0.0) + jnp.where(rid == row0 + 1, hid[1:2], 0.0)
        for b in range(4):
            sb[xt, b] = v[b * 8 : b * 8 + 8].astype(BF16)
        for dl in (2, 1, 3, 0):
            if (dx, dl) == (0, 0):
                continue
            i = tp_offs.index((dx, dl))
            lt = (zl + dl) % 4
            cp = remote(sb.at[xt, lt], rb.at[i], bs.at[i], br.at[i], dev(xt, y, zh * 4 + lt, c))
            cp.start()
            sends.append(cp)
            bcp.append(cp)
    v = sb[x, zl].astype(F32)
    for i in range(15):
        bcp[i].wait_recv()
        v = v + rb[i].astype(F32)
    ia = x * (1 - c) + y * c
    ib = y * (1 - c) + x * c
    g[c, ia, ib, z] = v.astype(BF16)

    for k in range(1, 8):
        own_piece = g.at[c, ia, ib, z]
        cp = remote(own_piece, own_piece, c1s.at[k - 1], c1r.at[k - 1], dev(x, y, (z + k) % 8, c))
        cp.start()
        sends.append(cp)
    for k in range(1, 8):
        piece = g.at[c, ia, ib, (z + 8 - k) % 8]
        remote(piece, piece, c1s.at[k - 1], c1r.at[k - 1], sib).wait_recv()
    for k in (2, 1, 3):
        run = g.at[c, ia, ib]
        cp = remote(
            run, run, c2s.at[k - 1], c2r.at[k - 1], dev((x + k * c) % 4, (y + k * (1 - c)) % 4, z, c)
        )
        cp.start()
        sends.append(cp)
    for k in (1, 3, 2):
        run = g.at[c, ia, (ib + 4 - k) % 4]
        remote(run, run, c2s.at[k - 1], c2r.at[k - 1], sib).wait_recv()
    for k in (2, 1, 3):
        run = g.at[c, ia]
        cp = remote(
            run, run, c3s.at[k - 1], c3r.at[k - 1], dev((x + k * (1 - c)) % 4, (y + k * c) % 4, z, c)
        )
        cp.start()
        sends.append(cp)
    cp = remote(g.at[c, ia], g.at[c, ia], cfs.at[0], cfr.at[0], sib)
    cp.start()
    sends.append(cp)
    for k in (1, 3, 2):
        run = g.at[c, (ia + 4 - k) % 4]
        remote(run, run, c3s.at[k - 1], c3r.at[k - 1], sib).wait_recv()
        cp = remote(run, run, cfs.at[k], cfr.at[k], sib)
        cp.start()
        sends.append(cp)
    ja = x * c + y * (1 - c)
    for k in (0, 1, 3, 2):
        run = g.at[1 - c, (ja + 4 - k) % 4]
        remote(run, run, cfs.at[k], cfr.at[k], sib).wait_recv()

    for load in loads[2:]:
        load.wait()
    row_y = lax.broadcasted_iota(jnp.int32, (256, UNITS), 0) // 64
    row_class = jnp.where(
        row_y == 0, wc_ref[0], jnp.where(row_y == 1, wc_ref[1], jnp.where(row_y == 2, wc_ref[2], wc_ref[3]))
    )
    unit = (seq * 16 + tp) * UNITS + lax.broadcasted_iota(jnp.int32, (256, UNITS), 1)
    active = unit < (row_class + 1) * (FF // WIDTHS)
    for plane in range(2):
        accg[...] = jnp.zeros_like(accg)
        accu[...] = jnp.zeros_like(accu)

        def quarter(k, ss, plane=plane):
            v = g[0, k] if plane == 0 else g[1, :, k]
            f = v.astype(F32).reshape(256, QD)
            at = pl.ds(pl.multiple_of(k * QD, 128), QD)
            u = (f * gain_ref[:, at]).astype(BF16)
            accg[...] += dot_nt(u, wg_v[:, at])
            accu[...] += dot_nt(u, wu_v[:, at])
            return ss + jnp.sum(f * f, axis=1, keepdims=True)

        ss = lax.fori_loop(0, 4, quarter, jnp.zeros((256, 1), F32))
        scale = lax.rsqrt(ss * (1.0 / D) + EPS)
        gate = accg[...] * scale
        up = accu[...] * scale
        act = 0.5 * gate * (1.0 + jnp.tanh(0.7978845608028654 * (gate + 0.044715 * gate * gate * gate)))
        hs[...] = jnp.where(active, act * up, 0.0).astype(BF16)

        def down(k, _, plane=plane):
            at = pl.ds(pl.multiple_of(k * QD, 128), QD)
            v = jnp.dot(hs[...], wd_v[:, at], preferred_element_type=F32)
            v = v.astype(BF16).reshape(4, 2, 4, 8, QD)
            for b in range(4):
                if plane == 0:
                    p[0, b, :, :, :, at] = v[:, :, b]
                else:
                    p[1, :, b, :, :, at] = v[:, :, b]
            return 0

        lax.fori_loop(0, 4, down, 0)

    for k in (2, 1, 3, 0):
        at = (ja + k) % 4
        cp = remote(p.at[1 - c, at], r.at[k], d0s.at[k], d0r.at[k], sib)
        cp.start()
        sends.append(cp)
    for k in (2, 1, 3, 0):
        at = (ia + k) % 4
        remote(p.at[c, at], r.at[k], d0s.at[k], d0r.at[k], sib).wait_recv()

        def add(i, _, at=at, k=k):
            b, h = i // 2, i % 2
            p[c, at, b, h] = (p[c, at, b, h].astype(F32) + r[k, b, h].astype(F32)).astype(BF16)
            return 0

        lax.fori_loop(0, 8, add, 0)
        if k:
            cp = remote(
                p.at[c, at], rx1.at[k - 1], d1s.at[k - 1], d1r.at[k - 1],
                dev((x + k * (1 - c)) % 4, (y + k * c) % 4, z, c),
            )
            cp.start()
            sends.append(cp)

    rid8 = lax.broadcasted_iota(jnp.int32, (8, QD), 0)
    for k in range(4):
        v = g[c, k * (1 - c) + y * c, y * (1 - c) + k * c, zh * 4 + x].astype(F32)
        r0 = jnp.sum(jnp.where(rid8 == zl * 2, v, 0.0), axis=0, keepdims=True)
        r1 = jnp.sum(jnp.where(rid8 == zl * 2 + 1, v, 0.0), axis=0, keepdims=True)
        res[pl.ds(0, 1), pl.ds(k * QD, QD)] = r0
        res[pl.ds(1, 1), pl.ds(k * QD, QD)] = r1

    for k in (1, 3, 2):
        remote(p.at[c, ia], rx1.at[k - 1], d1s.at[k - 1], d1r.at[k - 1], sib).wait_recv()
    for k in (2, 1, 3, 0):
        at = (ib + k) % 4
        for h in range(2):
            v = p[c, ia, at, h].astype(F32)
            for j in range(3):
                v = v + rx1[j, at, h].astype(F32)
            t[at, h] = v.astype(BF16)
        if k:
            cp = remote(
                t.at[at], rx2.at[k - 1], d2s.at[k - 1], d2r.at[k - 1],
                dev((x + k * c) % 4, (y + k * (1 - c)) % 4, z, c),
            )
            cp.start()
            sends.append(cp)
    for k in (1, 3, 2):
        remote(t.at[ib], rx2.at[k - 1], d2s.at[k - 1], d2r.at[k - 1], sib).wait_recv()
    for h in range(2):
        v = t[ib, h].astype(F32)
        for j in range(3):
            v = v + rx2[j, h].astype(F32)
        for b in range(4):
            zb[h * 4 + b] = v[b * 2 : b * 2 + 2].astype(BF16)
    d3 = []
    for k in (4, 3, 5, 2, 6, 1, 7):
        zt = (z + k) % 8
        cp = remote(zb.at[zt], rx3.at[k - 1], d3s.at[k - 1], d3r.at[k - 1], dev(x, y, zt, c))
        cp.start()
        sends.append(cp)
        d3.append(cp)
    v = zb[z].astype(F32)
    for cp in d3:
        cp.wait_recv()
    for k in range(7):
        v = v + rx3[k].astype(F32)
    out_ref[...] = (v + res[...]).astype(BF16)
    for cp in sends:
        cp.wait_send()


def body(
    hidden_in, query, kv_pool, kv_map, lengths, o_weight, norm_gain, width_class,
    gate_weight, up_weight, down_weight,
):
    vmem = pl.BlockSpec(memory_space=pltpu.VMEM)
    hbm = pl.BlockSpec(memory_space=pl.ANY)
    V, S = pltpu.VMEM, pltpu.SemaphoreType.DMA
    scratch = [
        V((4096, 128), BF16), V((256, D), BF16), V((UNITS, D), BF16), V((UNITS, D), BF16), V((UNITS, D), BF16),
        V((16, 32, 256), BF16),
        V((512, 512), BF16),
        V((512, 512), BF16),
        V((512, 256), BF16),
        V((512, 128), F32),
        V((512, 384), BF16),
        V((2, 8, 32, 384), BF16),
        V((8, 32, 384), BF16),
        V((7, 32, 384), BF16),
        V((4, 4, 8, QD), BF16),
        V((15, 8, QD), BF16),
        V((2, 4, 4, 8, 8, QD), BF16),
        V((512, 128), BF16),
        V((256, UNITS), F32), V((256, UNITS), F32),
        V((256, UNITS), BF16),
        V((2, 4, 4, 2, 8, D), BF16),
        V((4, 4, 2, 8, D), BF16),
        V((3, 4, 2, 8, D), BF16),
        V((4, 2, 8, D), BF16),
        V((3, 2, 8, D), BF16),
        V((8, 2, D), BF16),
        V((7, 2, D), BF16),
        V((2, D), F32),
        S((5,)),
        S((15,)), S((15,)), S((8,)), S((8,)), S((15,)), S((15,)),
        S((7,)), S((7,)), S((3,)), S((3,)), S((3,)), S((3,)), S((4,)), S((4,)),
        S((4,)), S((4,)), S((3,)), S((3,)), S((3,)), S((3,)), S((7,)), S((7,)),
    ]
    return pl.pallas_call(
        kernel,
        out_shape=jax.ShapeDtypeStruct((2, D), BF16),
        in_specs=[vmem, vmem, vmem, vmem, pl.BlockSpec(memory_space=pltpu.SMEM), vmem] + [hbm] * 5,
        out_specs=vmem,
        scratch_shapes=scratch,
        compiler_params=pltpu.CompilerParams(
            collective_id=0, has_side_effects=True, vmem_limit_bytes=56 << 20
        ),
        name="layer",
    )(
        hidden_in,
        query,
        kv_map.reshape(4, 128),
        lengths.reshape(4, 128),
        width_class,
        norm_gain.reshape(1, D),
        kv_pool.reshape(4096, 128),
        o_weight,
        jnp.transpose(gate_weight),
        jnp.transpose(up_weight),
        down_weight,
    )


def solution(mesh):
    placed = (
        P(("seq", "tp"), None),
        P("seq", "tp"),
        P("seq", None, "tp", None, None),
        P(None, "seq"),
        P(),
        P("tp", None),
        P(),
        P(),
        P(None, ("seq", "tp")),
        P(None, ("seq", "tp")),
        P(("seq", "tp"), None),
    )
    return jax.shard_map(
        body, mesh=mesh, in_specs=placed, out_specs=P(("seq", "tp"), None), check_vma=False
    )
```

time: 1230 us -> 125 us (0.10)
  waiting for transfers between devices: 1170 us -> 0 us
  Pallas kernels: 0 us -> 121 us
  matrix products: 16.2 us -> 0 us
  between operations: 13.9 us -> 0.01 us
    all_gather x1 -> x0, waiting for transfers between devices: 683 us -> none  [body(): lax.all_gather(normed, ('seq', 'tp'), axis=0, tiled=True)]
    unnamed x5 -> x0, waiting for transfers between devices: 456 us -> none
    pallas_call x0 -> x1, Pallas kernels: none -> 121 us  [body(): pl.pallas_call(kernel, out_shape=jax.ShapeDtypeStruct((2, D), BF16), in_s...]
    all_to_all x1 -> x0, waiting for transfers between devices: 26.7 us -> none  [body(): lax.all_to_all(picked[:, :, :, None], 'seq', split_axis=0, concat_axis=3,...]
    dot_general x5 -> x0, matrix products: 16.2 us -> none  [the longest x1 9.82 us: feed_forward(): return jnp.dot(hidden, down_weight, preferred_element_type=jnp.float32)]
  transfers between devices with their start and end apart: 4 -> 0, of which waited for: 4 -> 0; matrix products, arithmetic and copies ran while one was open for 0% -> 0% of each run, Pallas kernels for 0% -> 0%
where the time goes in v1:
time: 125 us; the launch traced here: 124 us
  Pallas kernels  121 us (97%)
  local copies, waits for them, and re-layouts  2.69 us (2%)
    pallas_call x1, Pallas kernels, body(): pl.pallas_call(kernel, out_shape=jax.ShapeDtypeStruct((2, D), BF16), in_s...  121 us

profile of v1, /device:TPU:8, one launch (start us, length us, event | category | flops | bytes accessed | tf_op | source)
XLA Modules:
  0.0 124.0 jit_solution(9922584249760836409)
XLA Ops:
  0.0 1.3 %reshape.14.gain_ref = f32[1,4608]{1,0:T(1,128)} reshape(f32[4608]{0:T(1024)} %param.17) | data formatting | bytes 36864 | tf_op jit(solution)/shard_map/reshape | solution.py:424
  1.3 121.3 %layer.1 = bf16[2,4608]{1,0:T(2,128)(2,1)} custom-call(bf16[2,4608]{1,0:T(2,128)(2,1)} %hid_ref.1, bf16[32,256]{1,0:T(8,128)(2,1)} %q_ref.1, s32[4,128]{1,0:T(4,128)} %bitcast.8, s32[4,128]{1,0:T(4,128)} %bitcast.9, s32[4]{0:T(128)} %wc_ref.1, f32[1,4608]{1,0:T(1,128)} %reshape.14.gain_ref, bf16[4096,128]{1,0:T(8,128)(2,1)} %bitcast.7, ...), custom_call_target="tpu_custom_call" | custom-call | tf_op jit(solution)/shard_map/layer/pallas_call | solution.py:408
  122.7 1.3 %copy.13 = bf16[2,4608]{1,0:T(2,128)(2,1)} copy(bf16[2,4608]{1,0:T(2,128)(2,1)} %layer.1) | data formatting | bytes 36864

commit v2 on v1

--- a/solution.py
+++ b/solution.py
@@ -38,7 +38,7 @@
     hid_ref, q_ref, kvm_ref, len_ref, wc_ref, gain_ref, kv_hbm, ow_hbm, wg_hbm, wu_hbm, wd_hbm,
     out_ref,
     kv_v, ow_v, wg_v, wu_v, wd_v,
-    qb, oh, oht, qs, ls, ns, nb, nr, nrx, sb, rb, g, xs, accg, accu, hs, p, r, rx1, t, rx2, zb, rx3, res,
+    qb, oh, oht, qs, ls, ns, nb, nr, nrx, sb, rb, g, xs, accg, accu, ssq, hs, p, r, rx1, t, rx2, zb, rx3, res,
     lsem, a1s, a1r, a3s, a3r, bs, br, c1s, c1r, c2s, c2r, c3s, c3r, cfs, cfr,
     d0s, d0r, d1s, d1r, d2s, d2r, d3s, d3r,
 ):
@@ -142,7 +142,7 @@
         ns[rows, pl.ds(256, 128)] = jnp.where(lane < 64, hi, both - hi).astype(BF16)
         return 0
 
-    lax.fori_loop(0, 16, attend, 0)
+    lax.fori_loop(0, 16, attend, 0, unroll=4)
 
     for k in range(4):
         v = jnp.dot(
@@ -212,145 +212,202 @@
     for i in range(15):
         bcp[i].wait_recv()
         v = v + rb[i].astype(F32)
-    ia = x * (1 - c) + y * c
-    ib = y * (1 - c) + x * c
-    g[c, ia, ib, z] = v.astype(BF16)
-
-    for k in range(1, 8):
-        own_piece = g.at[c, ia, ib, z]
-        cp = remote(own_piece, own_piece, c1s.at[k - 1], c1r.at[k - 1], dev(x, y, (z + k) % 8, c))
+    outer, inner = (x, y), (y, x)
+    own_piece = g.at[c, zh, x * (1 - zh) + y * zh, y * (1 - zh) + x * zh, zl]
+    own_piece[...] = v.astype(BF16)
+
+    def step(h, along_outer, k):
+        if (h == 0) == along_outer:
+            return dev((x + k) % 4, y, z, c)
+        return dev(x, (y + k) % 4, z, c)
+
+    def push(src, dst, ssem, rsem, to):
+        cp = remote(src, dst, ssem, rsem, to)
         cp.start()
         sends.append(cp)
-    for k in range(1, 8):
-        piece = g.at[c, ia, ib, (z + 8 - k) % 8]
-        remote(piece, piece, c1s.at[k - 1], c1r.at[k - 1], sib).wait_recv()
-    for k in (2, 1, 3):
-        run = g.at[c, ia, ib]
-        cp = remote(
-            run, run, c2s.at[k - 1], c2r.at[k - 1], dev((x + k * c) % 4, (y + k * (1 - c)) % 4, z, c)
-        )
-        cp.start()
-        sends.append(cp)
-    for k in (1, 3, 2):
-        run = g.at[c, ia, (ib + 4 - k) % 4]
-        remote(run, run, c2s.at[k - 1], c2r.at[k - 1], sib).wait_recv()
-    for k in (2, 1, 3):
-        run = g.at[c, ia]
-        cp = remote(
-            run, run, c3s.at[k - 1], c3r.at[k - 1], dev((x + k * (1 - c)) % 4, (y + k * c) % 4, z, c)
-        )
-        cp.start()
-        sends.append(cp)
-    cp = remote(g.at[c, ia], g.at[c, ia], cfs.at[0], cfr.at[0], sib)
-    cp.start()
-    sends.append(cp)
-    for k in (1, 3, 2):
-        run = g.at[c, (ia + 4 - k) % 4]
-        remote(run, run, c3s.at[k - 1], c3r.at[k - 1], sib).wait_recv()
-        cp = remote(run, run, cfs.at[k], cfr.at[k], sib)
-        cp.start()
-        sends.append(cp)
-    ja = x * c + y * (1 - c)
-    for k in (0, 1, 3, 2):
-        run = g.at[1 - c, (ja + 4 - k) % 4]
-        remote(run, run, cfs.at[k], cfr.at[k], sib).wait_recv()
-
+
+    for k in (4, 3, 5, 2, 6, 1, 7):
+        push(own_piece, own_piece, c1s.at[k - 1], c1r.at[k - 1], dev(x, y, (z + k) % 8, c))
+    accg[...] = jnp.zeros_like(accg)
+    accu[...] = jnp.zeros_like(accu)
+    ssq[...] = jnp.zeros_like(ssq)
     for load in loads[2:]:
         load.wait()
-    row_y = lax.broadcasted_iota(jnp.int32, (256, UNITS), 0) // 64
+    for k in (1, 7, 2, 6, 3, 5, 4):
+        frm = (z + 8 - k) % 8
+        fh = frm // 4
+        piece = g.at[c, fh, x * (1 - fh) + y * fh, y * (1 - fh) + x * fh, frm % 4]
+        remote(piece, piece, c1s.at[k - 1], c1r.at[k - 1], sib).wait_recv()
+    for k in (1, 3, 2):
+        for h in range(2):
+            run = g.at[c, h, outer[h], inner[h]]
+            push(run, run, c2s.at[h, k - 1], c2r.at[h, k - 1], step(h, False, k))
+    for k in (1, 3, 2):
+        for h in range(2):
+            run = g.at[c, h, outer[h], inner[h]]
+            push(run, run, c3s.at[h, 0, k - 1], c3r.at[h, 0, k - 1], step(h, True, k))
+    for j in (1, 3, 2):
+        for h in range(2):
+            run = g.at[c, h, outer[h], (inner[h] + 4 - j) % 4]
+            remote(run, run, c2s.at[h, j - 1], c2r.at[h, j - 1], sib).wait_recv()
+            for k in (1, 3):
+                push(run, run, c3s.at[h, j, k - 1], c3r.at[h, j, k - 1], step(h, True, k))
+    for j in (1, 3, 2):
+        for h in range(2):
+            run = g.at[c, h, outer[h], (inner[h] + 4 - j) % 4]
+            push(run, run, c3s.at[h, j, 1], c3r.at[h, j, 1], step(h, True, 2))
+    for h in range(2):
+        run = g.at[c, h, outer[h]]
+        push(run, run, cfs.at[h, 0], cfr.at[h, 0], sib)
+
+    def partial(h, f, xq, at):
+        cols = pl.ds(pl.multiple_of(xq * QD, 128), QD)
+        u = (f * gain_ref[:, cols]).astype(BF16)
+        accg[h, at, :] += dot_nt(u, wg_v[:, cols])
+        accu[h, at, :] += dot_nt(u, wu_v[:, cols])
+        ssq[h, at, :] += jnp.sum(f * f, axis=1, keepdims=True)
+
+    def first_half(plane, xq):
+        f = g[plane, 0, xq].astype(F32).reshape(128, QD)
+        partial(0, f, xq, pl.ds(pl.multiple_of(plane * 128, 128), 128))
+
+    def from_sibling(h, k):
+        run = g.at[1 - c, h, (outer[h] + 4 - k) % 4]
+        remote(run, run, cfs.at[h, k], cfr.at[h, k], sib).wait_recv()
+
+    first_half(c, x)
+    for h in range(2):
+        from_sibling(h, 0)
+    first_half(1 - c, x)
+    for k in (1, 3, 2):
+        for h in range(2):
+            for j in (0, 1, 3, 2):
+                run = g.at[c, h, (outer[h] + 4 - k) % 4, (inner[h] + 4 - j) % 4]
+                remote(run, run, c3s.at[h, j, k - 1], c3r.at[h, j, k - 1], sib).wait_recv()
+            run = g.at[c, h, (outer[h] + 4 - k) % 4]
+            push(run, run, cfs.at[h, k], cfr.at[h, k], sib)
+        first_half(c, (x + 4 - k) % 4)
+        if k == 2:
+            from_sibling(1, k)
+        for h in range(2):
+            if (h, k) != (1, 2):
+                from_sibling(h, k)
+        first_half(1 - c, (x + 4 - k) % 4)
+
+    def second_half(xq, _):
+        f = g[:, 1, :, xq].astype(F32).reshape(256, QD)
+        partial(1, f, xq, pl.ds(0, 256))
+        return 0
+
+    lax.fori_loop(0, 4, second_half, 0)
+
+    row_y = (lax.broadcasted_iota(jnp.int32, (128, UNITS), 0) >> 5) & 3
     row_class = jnp.where(
         row_y == 0, wc_ref[0], jnp.where(row_y == 1, wc_ref[1], jnp.where(row_y == 2, wc_ref[2], wc_ref[3]))
     )
-    unit = (seq * 16 + tp) * UNITS + lax.broadcasted_iota(jnp.int32, (256, UNITS), 1)
+    unit = (seq * 16 + tp) * UNITS + lax.broadcasted_iota(jnp.int32, (128, UNITS), 1)
     active = unit < (row_class + 1) * (FF // WIDTHS)
-    for plane in range(2):
-        accg[...] = jnp.zeros_like(accg)
-        accu[...] = jnp.zeros_like(accu)
-
-        def quarter(k, ss, plane=plane):
-            v = g[0, k] if plane == 0 else g[1, :, k]
-            f = v.astype(F32).reshape(256, QD)
-            at = pl.ds(pl.multiple_of(k * QD, 128), QD)
-            u = (f * gain_ref[:, at]).astype(BF16)
-            accg[...] += dot_nt(u, wg_v[:, at])
-            accu[...] += dot_nt(u, wu_v[:, at])
-            return ss + jnp.sum(f * f, axis=1, keepdims=True)
-
-        ss = lax.fori_loop(0, 4, quarter, jnp.zeros((256, 1), F32))
-        scale = lax.rsqrt(ss * (1.0 / D) + EPS)
-        gate = accg[...] * scale
-        up = accu[...] * scale
+
+    def activate(i, _):
+        h, plane = i // 2, i % 2
+        at = pl.ds(pl.multiple_of(plane * 128, 128), 128)
+        scale = lax.rsqrt(ssq[h, at, :] * (1.0 / D) + EPS)
+        gate = accg[h, at, :] * scale
+        up = accu[h, at, :] * scale
         act = 0.5 * gate * (1.0 + jnp.tanh(0.7978845608028654 * (gate + 0.044715 * gate * gate * gate)))
-        hs[...] = jnp.where(active, act * up, 0.0).astype(BF16)
-
-        def down(k, _, plane=plane):
-            at = pl.ds(pl.multiple_of(k * QD, 128), QD)
-            v = jnp.dot(hs[...], wd_v[:, at], preferred_element_type=F32)
-            v = v.astype(BF16).reshape(4, 2, 4, 8, QD)
+        hs[plane, pl.ds(pl.multiple_of(h * 128, 128), 128), :] = jnp.where(active, act * up, 0.0).astype(BF16)
+        return 0
+
+    lax.fori_loop(0, 4, activate, 0)
+
+    def down(plane, k):
+        cols = pl.ds(pl.multiple_of(k * QD, 128), QD)
+        v = jnp.dot(hs[plane], wd_v[:, cols], preferred_element_type=F32)
+        v = v.astype(BF16).reshape(2, 4, 4, 8, QD)
+        for w in range(4):
+            p[plane, k, 0, w] = v[0, :, w]
+        p[plane, k, 1] = v[1]
+
+    def d0(k):
+        return remote(p.at[1 - c, k], r.at[k], d0s.at[k], d0r.at[k], sib)
+
+    def d1(k, h, off):
+        return remote(
+            p.at[c, k, h, (outer[h] + off) % 4], rx1.at[k, h, off - 1],
+            d1s.at[k, h, off - 1], d1r.at[k, h, off - 1], step(h, True, off),
+        )
+
+    def d2(k, h, off):
+        return remote(
+            t.at[k, h, (inner[h] + off) % 4], rx2.at[k, h, off - 1],
+            d2s.at[k, h, off - 1], d2r.at[k, h, off - 1], step(h, False, off),
+        )
+
+    def pair(k):
+        d0(k).wait_recv()
+
+        def add(i, _):
+            h, a = i // 4, i % 4
+            p[c, k, h, a] = (p[c, k, h, a].astype(F32) + r[k, h, a].astype(F32)).astype(BF16)
+            return 0
+
+        lax.fori_loop(0, 8, add, 0)
+        for off in (2, 1, 3):
+            for h in range(2):
+                d1(k, h, off).start()
+
+    def produce(k, _):
+        down(1 - c, k)
+        d0(k).start()
+        down(c, k)
+
+        @pl.when(k > 0)
+        def _():
+            pair(k - 1)
+
+        return 0
+
+    lax.fori_loop(0, 4, produce, 0)
+    pair(3)
+
+    rid8 = lax.broadcasted_iota(jnp.int32, (8, QD), 0)
+
+    def own_rows(k, _):
+        v = g[c, zh, k * (1 - zh) + y * zh, y * (1 - zh) + k * zh, x].astype(F32)
+        cols = pl.ds(pl.multiple_of(k * QD, 128), QD)
+        res[pl.ds(0, 1), cols] = jnp.sum(jnp.where(rid8 == zl * 2, v, 0.0), axis=0, keepdims=True)
+        res[pl.ds(1, 1), cols] = jnp.sum(jnp.where(rid8 == zl * 2 + 1, v, 0.0), axis=0, keepdims=True)
+        return 0
+
+    lax.fori_loop(0, 4, own_rows, 0)
+
+    def outer_sum(k, _):
+        for h in range(2):
+            for off in (1, 3, 2):
+                d1(k, h, off).wait_recv()
+            v = p[c, k, h, outer[h]].astype(F32)
+            for j in range(3):
+                v = v + rx1[k, h, j].astype(F32)
+            t[k, h] = v.astype(BF16)
+            for off in (2, 1, 3):
+                d2(k, h, off).start()
+        return 0
+
+    lax.fori_loop(0, 4, outer_sum, 0)
+
+    def inner_sum(k, _):
+        cols = pl.ds(pl.multiple_of(k * QD, 128), QD)
+        for h in range(2):
+            for off in (1, 3, 2):
+                d2(k, h, off).wait_recv()
+            v = t[k, h, inner[h]].astype(F32)
+            for j in range(3):
+                v = v + rx2[k, h, j].astype(F32)
             for b in range(4):
-                if plane == 0:
-                    p[0, b, :, :, :, at] = v[:, :, b]
-                else:
-                    p[1, :, b, :, :, at] = v[:, :, b]
-            return 0
-
-        lax.fori_loop(0, 4, down, 0)
-
-    for k in (2, 1, 3, 0):
-        at = (ja + k) % 4
-        cp = remote(p.at[1 - c, at], r.at[k], d0s.at[k], d0r.at[k], sib)
-        cp.start()
-        sends.append(cp)
-    for k in (2, 1, 3, 0):
-        at = (ia + k) % 4
-        remote(p.at[c, at], r.at[k], d0s.at[k], d0r.at[k], sib).wait_recv()
-
-        def add(i, _, at=at, k=k):
-            b, h = i // 2, i % 2
-            p[c, at, b, h] = (p[c, at, b, h].astype(F32) + r[k, b, h].astype(F32)).astype(BF16)
-            return 0
-
-        lax.fori_loop(0, 8, add, 0)
-        if k:
-            cp = remote(
-                p.at[c, at], rx1.at[k - 1], d1s.at[k - 1], d1r.at[k - 1],
-                dev((x + k * (1 - c)) % 4, (y + k * c) % 4, z, c),
-            )
-            cp.start()
-            sends.append(cp)
-
-    rid8 = lax.broadcasted_iota(jnp.int32, (8, QD), 0)
-    for k in range(4):
-        v = g[c, k * (1 - c) + y * c, y * (1 - c) + k * c, zh * 4 + x].astype(F32)
-        r0 = jnp.sum(jnp.where(rid8 == zl * 2, v, 0.0), axis=0, keepdims=True)
-        r1 = jnp.sum(jnp.where(rid8 == zl * 2 + 1, v, 0.0), axis=0, keepdims=True)
-        res[pl.ds(0, 1), pl.ds(k * QD, QD)] = r0
-        res[pl.ds(1, 1), pl.ds(k * QD, QD)] = r1
-
-    for k in (1, 3, 2):
-        remote(p.at[c, ia], rx1.at[k - 1], d1s.at[k - 1], d1r.at[k - 1], sib).wait_recv()
-    for k in (2, 1, 3, 0):
-        at = (ib + k) % 4
-        for h in range(2):
-            v = p[c, ia, at, h].astype(F32)
-            for j in range(3):
-                v = v + rx1[j, at, h].astype(F32)
-            t[at, h] = v.astype(BF16)
-        if k:
-            cp = remote(
-                t.at[at], rx2.at[k - 1], d2s.at[k - 1], d2r.at[k - 1],
-                dev((x + k * c) % 4, (y + k * (1 - c)) % 4, z, c),
-            )
-            cp.start()
-            sends.append(cp)
-    for k in (1, 3, 2):
-        remote(t.at[ib], rx2.at[k - 1], d2s.at[k - 1], d2r.at[k - 1], sib).wait_recv()
-    for h in range(2):
-        v = t[ib, h].astype(F32)
-        for j in range(3):
-            v = v + rx2[j, h].astype(F32)
-        for b in range(4):
-            zb[h * 4 + b] = v[b * 2 : b * 2 + 2].astype(BF16)
+                zb[h * 4 + b, :, cols] = v[b * 2 : b * 2 + 2].astype(BF16)
+        return 0
+
+    lax.fori_loop(0, 4, inner_sum, 0)
     d3 = []
     for k in (4, 3, 5, 2, 6, 1, 7):
         zt = (z + k) % 8
@@ -358,14 +415,24 @@
         cp.start()
         sends.append(cp)
         d3.append(cp)
-    v = zb[z].astype(F32)
+    v = zb[z].astype(F32) + res[...]
     for cp in d3:
         cp.wait_recv()
     for k in range(7):
         v = v + rx3[k].astype(F32)
-    out_ref[...] = (v + res[...]).astype(BF16)
+    out_ref[...] = v.astype(BF16)
     for cp in sends:
         cp.wait_send()
+
+    def drain(k, _):
+        d0(k).wait_send()
+        for h in range(2):
+            for off in (1, 2, 3):
+                d1(k, h, off).wait_send()
+                d2(k, h, off).wait_send()
+        return 0
+
+    lax.fori_loop(0, 4, drain, 0)
 
 
 def body(
@@ -388,22 +455,23 @@
         V((7, 32, 384), BF16),
         V((4, 4, 8, QD), BF16),
         V((15, 8, QD), BF16),
-        V((2, 4, 4, 8, 8, QD), BF16),
+        V((2, 2, 4, 4, 4, 8, QD), BF16),
         V((512, 128), BF16),
-        V((256, UNITS), F32), V((256, UNITS), F32),
-        V((256, UNITS), BF16),
-        V((2, 4, 4, 2, 8, D), BF16),
-        V((4, 4, 2, 8, D), BF16),
-        V((3, 4, 2, 8, D), BF16),
-        V((4, 2, 8, D), BF16),
-        V((3, 2, 8, D), BF16),
+        V((2, 256, UNITS), F32), V((2, 256, UNITS), F32),
+        V((2, 256, 1), F32),
+        V((2, 256, UNITS), BF16),
+        V((2, 4, 2, 4, 4, 8, QD), BF16),
+        V((4, 2, 4, 4, 8, QD), BF16),
+        V((4, 2, 3, 4, 8, QD), BF16),
+        V((4, 2, 4, 8, QD), BF16),
+        V((4, 2, 3, 8, QD), BF16),
         V((8, 2, D), BF16),
         V((7, 2, D), BF16),
         V((2, D), F32),
         S((5,)),
         S((15,)), S((15,)), S((8,)), S((8,)), S((15,)), S((15,)),
-        S((7,)), S((7,)), S((3,)), S((3,)), S((3,)), S((3,)), S((4,)), S((4,)),
-        S((4,)), S((4,)), S((3,)), S((3,)), S((3,)), S((3,)), S((7,)), S((7,)),
+        S((7,)), S((7,)), S((2, 3)), S((2, 3)), S((2, 4, 3)), S((2, 4, 3)), S((2, 4)), S((2, 4)),
+        S((4,)), S((4,)), S((4, 2, 3)), S((4, 2, 3)), S((4, 2, 3)), S((4, 2, 3)), S((7,)), S((7,)),
     ]
     return pl.pallas_call(
         kernel,

time: 125 us -> 104 us (0.83)
  Pallas kernels: 121 us -> 101 us
    pallas_call x1, Pallas kernels: 121 us -> 101 us  [body(): pl.pallas_call(kernel, out_shape=jax.ShapeDtypeStruct((2, D), BF16), in_s...]
where the time goes in v2:
time: 104 us
  Pallas kernels  101 us (97%)
  local copies, waits for them, and re-layouts  2.69 us (3%)
    pallas_call x1, Pallas kernels, body(): pl.pallas_call(kernel, out_shape=jax.ShapeDtypeStruct((2, D), BF16), in_s...  101 us

profile of v2, /device:TPU:8, one launch (start us, length us, event | category | flops | bytes accessed | tf_op | source)
XLA Modules:
  0.0 104.1 jit_solution(18247273310403535676)
XLA Ops:
  0.0 1.3 %reshape.14.gain_ref = f32[1,4608]{1,0:T(1,128)} reshape(f32[4608]{0:T(1024)} %param.17) | data formatting | bytes 36864 | tf_op jit(solution)/shard_map/reshape | solution.py:492
  1.3 101.4 %layer.1 = bf16[2,4608]{1,0:T(2,128)(2,1)} custom-call(bf16[2,4608]{1,0:T(2,128)(2,1)} %hid_ref.1, bf16[32,256]{1,0:T(8,128)(2,1)} %q_ref.1, s32[4,128]{1,0:T(4,128)} %bitcast.8, s32[4,128]{1,0:T(4,128)} %bitcast.9, s32[4]{0:T(128)} %wc_ref.1, f32[1,4608]{1,0:T(1,128)} %reshape.14.gain_ref, bf16[4096,128]{1,0:T(8,128)(2,1)} %bitcast.7, ...), custom_call_target="tpu_custom_call" | custom-call | tf_op jit(solution)/shard_map/layer/pallas_call | solution.py:476
  102.8 1.3 %copy.13 = bf16[2,4608]{1,0:T(2,128)(2,1)} copy(bf16[2,4608]{1,0:T(2,128)(2,1)} %layer.1) | data formatting | bytes 36864

commit v3 on v2

--- a/solution.py
+++ b/solution.py
@@ -37,10 +37,10 @@
 def kernel(
     hid_ref, q_ref, kvm_ref, len_ref, wc_ref, gain_ref, kv_hbm, ow_hbm, wg_hbm, wu_hbm, wd_hbm,
     out_ref,
-    kv_v, ow_v, wg_v, wu_v, wd_v,
-    qb, oh, oht, qs, ls, ns, nb, nr, nrx, sb, rb, g, xs, accg, accu, ssq, hs, p, r, rx1, t, rx2, zb, rx3, res,
-    lsem, a1s, a1r, a3s, a3r, bs, br, c1s, c1r, c2s, c2r, c3s, c3r, cfs, cfr,
-    d0s, d0r, d1s, d1r, d2s, d2r, d3s, d3r,
+    kv_v, ow_v, wgu_v, wd_v,
+    qb, oh, oht, qs, ls, ns, nb, nr, nrx, sb, rb, g, xs, acc, ssq, hs, p, rx1, t, rx2, zb, rx3, res, gain, kvt, vs,
+    lsem, a1s, a1r, a3s, a3r, bs, br, c1s, c1r, c2s, c2r, c3s, c3r,
+    wxs, wxr, d1s, d1r, d2s, d2r, d3s, d3r,
 ):
     seq = lax.axis_index("seq")
     tp = lax.axis_index("tp")
@@ -62,9 +62,9 @@
     loads = [
         pltpu.make_async_copy(kv_hbm, kv_v, lsem.at[0]),
         pltpu.make_async_copy(ow_hbm, ow_v, lsem.at[1]),
-        pltpu.make_async_copy(wg_hbm, wg_v, lsem.at[2]),
-        pltpu.make_async_copy(wu_hbm, wu_v, lsem.at[3]),
-        pltpu.make_async_copy(wd_hbm, wd_v, lsem.at[4]),
+        pltpu.make_async_copy(wg_hbm, wgu_v.at[0, c], lsem.at[2]),
+        pltpu.make_async_copy(wu_hbm, wgu_v.at[1, c], lsem.at[3]),
+        pltpu.make_async_copy(wd_hbm, wd_v.at[c], lsem.at[4]),
     ]
     for load in loads:
         load.start()
@@ -96,8 +96,21 @@
         xs[pl.ds(j * 128, 128), pl.ds(0, 128)] = jnp.transpose(
             jnp.broadcast_to(lrow, (128, 128))
         ).astype(BF16)
+    for j in range(36):
+        gain[:, pl.ds(j * 128, 128)] = gain_ref[pl.ds(j, 1), :]
     ls[...] = jnp.dot(oh[...], xs[:, pl.ds(0, 128)], preferred_element_type=F32)
 
+    loads[0].wait()
+
+    def prepare(blk, _):
+        rows = pl.ds(pl.multiple_of(blk * 256, 256), 256)
+        block = kv_v[rows, :].astype(F32)
+        kvt[:, rows] = jnp.transpose(block).astype(BF16)
+        vs[rows, pl.ds(0, 128)] = pltpu.roll(block, 252, 0).astype(BF16)
+        vs[rows, pl.ds(128, 128)] = jnp.ones((256, 128), BF16)
+        return 0
+
+    lax.fori_loop(0, 16, prepare, 0)
     for i, (dy, dh) in enumerate(seq_offs):
         frm = ((y - dy) % 4) * 4 + ((zh + dh) % 2) * 2 + c
         a = remote(q_ref, qb.at[frm], a1s.at[i], a1r.at[i], sib)
@@ -110,10 +123,16 @@
         frm = ((y - dy) % 4) * 4 + ((zh + dh) % 2) * 2 + (1 - c)
         remote(qb.at[frm], qb.at[frm], a1s.at[8 + i], a1r.at[8 + i], sib).wait_recv()
 
+    weights = [
+        remote(wg_hbm, wgu_v.at[0, c], wxs.at[0], wxr.at[0], sib),
+        remote(wu_hbm, wgu_v.at[1, c], wxs.at[1], wxr.at[1], sib),
+        remote(wd_hbm, wd_v.at[c], wxs.at[2], wxr.at[2], sib),
+    ]
+    sends += weights
+    weights[0].start()
     qs[...] = jnp.dot(
         oh[...], qb[...].reshape(512, 256), preferred_element_type=F32
     ).astype(BF16)
-    loads[0].wait()
 
     first = seq * 4
     a_id = lax.broadcasted_iota(jnp.int32, (64, 256), 0) & 31
@@ -124,19 +143,20 @@
 
     def attend(blk, _):
         rows = pl.ds(pl.multiple_of(blk * 32, 32), 32)
-        keys = kv_v[pl.ds(pl.multiple_of(blk * 256, 256), 256), :]
+        span = pl.ds(pl.multiple_of(blk * 256, 256), 256)
         qq = jnp.concatenate([qs[rows, pl.ds(0, 128)], qs[rows, pl.ds(128, 128)]], axis=0)
-        s = dot_nt(qq, keys)
+        s = jnp.dot(qq, kvt[:, span], preferred_element_type=F32)
         e = jnp.exp(SOFTCAP * jnp.tanh(s * (QPRE ** (-0.5) / SOFTCAP)))
         lb = ls[rows, :]
         lb = jnp.concatenate([lb, lb], axis=0)
         lb = jnp.concatenate([lb, lb], axis=1)
         w = jnp.where(own & (pos < lb), e, 0.0)
-        tot = jnp.sum(w, axis=1, keepdims=True)
-        wv = pltpu.roll(w, 4, 1).astype(BF16)
-        num = jnp.dot(wv, keys, preferred_element_type=F32)
-        ns[rows, pl.ds(0, 128)] = num[:32].astype(BF16)
-        ns[rows, pl.ds(128, 128)] = num[32:].astype(BF16)
+        low = w.astype(BF16)
+        rest = (w - low.astype(F32)).astype(BF16)
+        num = jnp.dot(jnp.concatenate([low, rest], axis=0), vs[span, :], preferred_element_type=F32)
+        ns[rows, pl.ds(0, 128)] = num[:32, :128].astype(BF16)
+        ns[rows, pl.ds(128, 128)] = num[32:64, :128].astype(BF16)
+        tot = num[:64, 128:] + num[64:, 128:]
         both = jnp.where((lane & 63) < 32, tot[:32], tot[32:])
         hi = both.astype(BF16).astype(F32)
         ns[rows, pl.ds(256, 128)] = jnp.where(lane < 64, hi, both - hi).astype(BF16)
@@ -178,6 +198,7 @@
         cp.start()
         sends.append(cp)
         a3.append(cp)
+    weights[1].start()
     total = nb[c, y * 2 + zh].astype(F32)
     for i in range(7):
         a3[i].wait_recv()
@@ -208,12 +229,13 @@
             cp.start()
             sends.append(cp)
             bcp.append(cp)
+    weights[2].start()
     v = sb[x, zl].astype(F32)
     for i in range(15):
         bcp[i].wait_recv()
         v = v + rb[i].astype(F32)
     outer, inner = (x, y), (y, x)
-    own_piece = g.at[c, zh, x * (1 - zh) + y * zh, y * (1 - zh) + x * zh, zl]
+    own_piece = g.at[zh, x * (1 - zh) + y * zh, y * (1 - zh) + x * zh, zl]
     own_piece[...] = v.astype(BF16)
 
     def step(h, along_outer, k):
@@ -228,112 +250,82 @@
 
     for k in (4, 3, 5, 2, 6, 1, 7):
         push(own_piece, own_piece, c1s.at[k - 1], c1r.at[k - 1], dev(x, y, (z + k) % 8, c))
-    accg[...] = jnp.zeros_like(accg)
-    accu[...] = jnp.zeros_like(accu)
+    acc[...] = jnp.zeros_like(acc)
     ssq[...] = jnp.zeros_like(ssq)
     for load in loads[2:]:
         load.wait()
+    for weight in weights:
+        weight.wait_recv()
     for k in (1, 7, 2, 6, 3, 5, 4):
         frm = (z + 8 - k) % 8
         fh = frm // 4
-        piece = g.at[c, fh, x * (1 - fh) + y * fh, y * (1 - fh) + x * fh, frm % 4]
+        piece = g.at[fh, x * (1 - fh) + y * fh, y * (1 - fh) + x * fh, frm % 4]
         remote(piece, piece, c1s.at[k - 1], c1r.at[k - 1], sib).wait_recv()
     for k in (1, 3, 2):
         for h in range(2):
-            run = g.at[c, h, outer[h], inner[h]]
+            run = g.at[h, outer[h], inner[h]]
             push(run, run, c2s.at[h, k - 1], c2r.at[h, k - 1], step(h, False, k))
     for k in (1, 3, 2):
         for h in range(2):
-            run = g.at[c, h, outer[h], inner[h]]
+            run = g.at[h, outer[h], inner[h]]
             push(run, run, c3s.at[h, 0, k - 1], c3r.at[h, 0, k - 1], step(h, True, k))
     for j in (1, 3, 2):
         for h in range(2):
-            run = g.at[c, h, outer[h], (inner[h] + 4 - j) % 4]
+            run = g.at[h, outer[h], (inner[h] + 4 - j) % 4]
             remote(run, run, c2s.at[h, j - 1], c2r.at[h, j - 1], sib).wait_recv()
             for k in (1, 3):
                 push(run, run, c3s.at[h, j, k - 1], c3r.at[h, j, k - 1], step(h, True, k))
     for j in (1, 3, 2):
         for h in range(2):
-            run = g.at[c, h, outer[h], (inner[h] + 4 - j) % 4]
+            run = g.at[h, outer[h], (inner[h] + 4 - j) % 4]
             push(run, run, c3s.at[h, j, 1], c3r.at[h, j, 1], step(h, True, 2))
-    for h in range(2):
-        run = g.at[c, h, outer[h]]
-        push(run, run, cfs.at[h, 0], cfr.at[h, 0], sib)
-
-    def partial(h, f, xq, at):
+
+    def partial(h, f, xq):
         cols = pl.ds(pl.multiple_of(xq * QD, 128), QD)
-        u = (f * gain_ref[:, cols]).astype(BF16)
-        accg[h, at, :] += dot_nt(u, wg_v[:, cols])
-        accu[h, at, :] += dot_nt(u, wu_v[:, cols])
-        ssq[h, at, :] += jnp.sum(f * f, axis=1, keepdims=True)
-
-    def first_half(plane, xq):
-        f = g[plane, 0, xq].astype(F32).reshape(128, QD)
-        partial(0, f, xq, pl.ds(pl.multiple_of(plane * 128, 128), 128))
-
-    def from_sibling(h, k):
-        run = g.at[1 - c, h, (outer[h] + 4 - k) % 4]
-        remote(run, run, cfs.at[h, k], cfr.at[h, k], sib).wait_recv()
-
-    first_half(c, x)
-    for h in range(2):
-        from_sibling(h, 0)
-    first_half(1 - c, x)
+        u = (f.astype(F32).reshape(128, QD) * gain[:, cols]).astype(BF16)
+        acc[h] += dot_nt(u, wgu_v[:, :, :, cols].reshape(4 * UNITS, QD))
+
+    def squares(h, f):
+        f = f.astype(F32).reshape(128, QD)
+        ssq[h] += jnp.sum(f * f, axis=1, keepdims=True)
+
+    def first_half(xq):
+        partial(0, g[0, xq], xq)
+        squares(0, g[0, xq])
+
+    first_half(x)
     for k in (1, 3, 2):
         for h in range(2):
             for j in (0, 1, 3, 2):
-                run = g.at[c, h, (outer[h] + 4 - k) % 4, (inner[h] + 4 - j) % 4]
+                run = g.at[h, (outer[h] + 4 - k) % 4, (inner[h] + 4 - j) % 4]
                 remote(run, run, c3s.at[h, j, k - 1], c3r.at[h, j, k - 1], sib).wait_recv()
-            run = g.at[c, h, (outer[h] + 4 - k) % 4]
-            push(run, run, cfs.at[h, k], cfr.at[h, k], sib)
-        first_half(c, (x + 4 - k) % 4)
-        if k == 2:
-            from_sibling(1, k)
-        for h in range(2):
-            if (h, k) != (1, 2):
-                from_sibling(h, k)
-        first_half(1 - c, (x + 4 - k) % 4)
+        first_half((x + 4 - k) % 4)
 
     def second_half(xq, _):
-        f = g[:, 1, :, xq].astype(F32).reshape(256, QD)
-        partial(1, f, xq, pl.ds(0, 256))
+        partial(1, g[1, :, xq], xq)
+        squares(1, g[1, :, xq])
         return 0
 
     lax.fori_loop(0, 4, second_half, 0)
 
-    row_y = (lax.broadcasted_iota(jnp.int32, (128, UNITS), 0) >> 5) & 3
+    row_y = lax.broadcasted_iota(jnp.int32, (128, 2 * UNITS), 0) >> 5
     row_class = jnp.where(
         row_y == 0, wc_ref[0], jnp.where(row_y == 1, wc_ref[1], jnp.where(row_y == 2, wc_ref[2], wc_ref[3]))
     )
-    unit = (seq * 16 + tp) * UNITS + lax.broadcasted_iota(jnp.int32, (128, UNITS), 1)
+    unit_id = lax.broadcasted_iota(jnp.int32, (128, 2 * UNITS), 1)
+    pair_base = ((seq - c) * 16 + tp) * UNITS
+    unit = pair_base + unit_id + jnp.where(unit_id >= UNITS, 15 * UNITS, 0)
     active = unit < (row_class + 1) * (FF // WIDTHS)
-
-    def activate(i, _):
-        h, plane = i // 2, i % 2
-        at = pl.ds(pl.multiple_of(plane * 128, 128), 128)
-        scale = lax.rsqrt(ssq[h, at, :] * (1.0 / D) + EPS)
-        gate = accg[h, at, :] * scale
-        up = accu[h, at, :] * scale
+    for h in range(2):
+        scale = lax.rsqrt(ssq[h] * (1.0 / D) + EPS)
+        gate = acc[h, :, : 2 * UNITS] * scale
+        up = acc[h, :, 2 * UNITS :] * scale
         act = 0.5 * gate * (1.0 + jnp.tanh(0.7978845608028654 * (gate + 0.044715 * gate * gate * gate)))
-        hs[plane, pl.ds(pl.multiple_of(h * 128, 128), 128), :] = jnp.where(active, act * up, 0.0).astype(BF16)
-        return 0
-
-    lax.fori_loop(0, 4, activate, 0)
-
-    def down(plane, k):
-        cols = pl.ds(pl.multiple_of(k * QD, 128), QD)
-        v = jnp.dot(hs[plane], wd_v[:, cols], preferred_element_type=F32)
-        v = v.astype(BF16).reshape(2, 4, 4, 8, QD)
-        for w in range(4):
-            p[plane, k, 0, w] = v[0, :, w]
-        p[plane, k, 1] = v[1]
-
-    def d0(k):
-        return remote(p.at[1 - c, k], r.at[k], d0s.at[k], d0r.at[k], sib)
+        hs[pl.ds(h * 128, 128), :] = jnp.where(active, act * up, 0.0).astype(BF16)
 
     def d1(k, h, off):
         return remote(
-            p.at[c, k, h, (outer[h] + off) % 4], rx1.at[k, h, off - 1],
+            p.at[k, h, (outer[h] + off) % 4], rx1.at[k, h, off - 1],
             d1s.at[k, h, off - 1], d1r.at[k, h, off - 1], step(h, True, off),
         )
 
@@ -343,37 +335,24 @@
             d2s.at[k, h, off - 1], d2r.at[k, h, off - 1], step(h, False, off),
         )
 
-    def pair(k):
-        d0(k).wait_recv()
-
-        def add(i, _):
-            h, a = i // 4, i % 4
-            p[c, k, h, a] = (p[c, k, h, a].astype(F32) + r[k, h, a].astype(F32)).astype(BF16)
-            return 0
-
-        lax.fori_loop(0, 8, add, 0)
+    def produce(k, _):
+        cols = pl.ds(pl.multiple_of(k * QD, 128), QD)
+        v = jnp.dot(hs[...], wd_v[:, :, cols].reshape(2 * UNITS, QD), preferred_element_type=F32)
+        v = v.astype(BF16).reshape(2, 4, 4, 8, QD)
+        for w in range(4):
+            p[k, 0, w] = v[0, :, w]
+        p[k, 1] = v[1]
         for off in (2, 1, 3):
             for h in range(2):
                 d1(k, h, off).start()
-
-    def produce(k, _):
-        down(1 - c, k)
-        d0(k).start()
-        down(c, k)
-
-        @pl.when(k > 0)
-        def _():
-            pair(k - 1)
-
         return 0
 
     lax.fori_loop(0, 4, produce, 0)
-    pair(3)
 
     rid8 = lax.broadcasted_iota(jnp.int32, (8, QD), 0)
 
     def own_rows(k, _):
-        v = g[c, zh, k * (1 - zh) + y * zh, y * (1 - zh) + k * zh, x].astype(F32)
+        v = g[zh, k * (1 - zh) + y * zh, y * (1 - zh) + k * zh, x].astype(F32)
         cols = pl.ds(pl.multiple_of(k * QD, 128), QD)
         res[pl.ds(0, 1), cols] = jnp.sum(jnp.where(rid8 == zl * 2, v, 0.0), axis=0, keepdims=True)
         res[pl.ds(1, 1), cols] = jnp.sum(jnp.where(rid8 == zl * 2 + 1, v, 0.0), axis=0, keepdims=True)
@@ -385,7 +364,7 @@
         for h in range(2):
             for off in (1, 3, 2):
                 d1(k, h, off).wait_recv()
-            v = p[c, k, h, outer[h]].astype(F32)
+            v = p[k, h, outer[h]].astype(F32)
             for j in range(3):
                 v = v + rx1[k, h, j].astype(F32)
             t[k, h] = v.astype(BF16)
@@ -425,7 +404,6 @@
         cp.wait_send()
 
     def drain(k, _):
-        d0(k).wait_send()
         for h in range(2):
             for off in (1, 2, 3):
                 d1(k, h, off).wait_send()
@@ -443,7 +421,7 @@
     hbm = pl.BlockSpec(memory_space=pl.ANY)
     V, S = pltpu.VMEM, pltpu.SemaphoreType.DMA
     scratch = [
-        V((4096, 128), BF16), V((256, D), BF16), V((UNITS, D), BF16), V((UNITS, D), BF16), V((UNITS, D), BF16),
+        V((4096, 128), BF16), V((256, D), BF16), V((2, 2, UNITS, D), BF16), V((2, UNITS, D), BF16),
         V((16, 32, 256), BF16),
         V((512, 512), BF16),
         V((512, 512), BF16),
@@ -455,12 +433,11 @@
         V((7, 32, 384), BF16),
         V((4, 4, 8, QD), BF16),
         V((15, 8, QD), BF16),
-        V((2, 2, 4, 4, 4, 8, QD), BF16),
+        V((2, 4, 4, 4, 8, QD), BF16),
         V((512, 128), BF16),
-        V((2, 256, UNITS), F32), V((2, 256, UNITS), F32),
-        V((2, 256, 1), F32),
-        V((2, 256, UNITS), BF16),
-        V((2, 4, 2, 4, 4, 8, QD), BF16),
+        V((2, 128, 4 * UNITS), F32),
+        V((2, 128, 1), F32),
+        V((256, 2 * UNITS), BF16),
         V((4, 2, 4, 4, 8, QD), BF16),
         V((4, 2, 3, 4, 8, QD), BF16),
         V((4, 2, 4, 8, QD), BF16),
@@ -468,10 +445,13 @@
         V((8, 2, D), BF16),
         V((7, 2, D), BF16),
         V((2, D), F32),
+        V((1, D), F32),
+        V((128, 4096), BF16),
+        V((4096, 256), BF16),
         S((5,)),
         S((15,)), S((15,)), S((8,)), S((8,)), S((15,)), S((15,)),
-        S((7,)), S((7,)), S((2, 3)), S((2, 3)), S((2, 4, 3)), S((2, 4, 3)), S((2, 4)), S((2, 4)),
-        S((4,)), S((4,)), S((4, 2, 3)), S((4, 2, 3)), S((4, 2, 3)), S((4, 2, 3)), S((7,)), S((7,)),
+        S((7,)), S((7,)), S((2, 3)), S((2, 3)), S((2, 4, 3)), S((2, 4, 3)),
+        S((3,)), S((3,)), S((4, 2, 3)), S((4, 2, 3)), S((4, 2, 3)), S((4, 2, 3)), S((7,)), S((7,)),
     ]
     return pl.pallas_call(
         kernel,
@@ -489,7 +469,7 @@
         kv_map.reshape(4, 128),
         lengths.reshape(4, 128),
         width_class,
-        norm_gain.reshape(1, D),
+        norm_gain.reshape(36, 128),
         kv_pool.reshape(4096, 128),
         o_weight,
         jnp.transpose(gate_weight),

time: 104 us -> 92.4 us (0.89)
  Pallas kernels: 101 us -> 90.5 us
  local copies, waits for them, and re-layouts: 2.69 us -> 1.34 us
    pallas_call x1, Pallas kernels: 101 us -> 90.5 us  [body(): pl.pallas_call(kernel, out_shape=jax.ShapeDtypeStruct((2, D), BF16), in_s...]
    reshape x1 -> x0, local copies, waits for them, and re-layouts: 1.35 us -> none  [body(): norm_gain.reshape(1, D)]
where the time goes in v3:
time: 92.4 us; the launch traced here: 91.8 us
  Pallas kernels  90.5 us (98%)
  local copies, waits for them, and re-layouts  1.34 us (1%)
    pallas_call x1, Pallas kernels, body(): pl.pallas_call(kernel, out_shape=jax.ShapeDtypeStruct((2, D), BF16), in_s...  90.5 us

profile of v3, /device:TPU:8, one launch (start us, length us, event | category | flops | bytes accessed | tf_op | source)
XLA Modules:
  0.0 91.8 jit_solution(1495120674653404409)
XLA Ops:
  0.0 90.5 %layer.1 = bf16[2,4608]{1,0:T(2,128)(2,1)} custom-call(bf16[2,4608]{1,0:T(2,128)(2,1)} %hid_ref.1, bf16[32,256]{1,0:T(8,128)(2,1)} %q_ref.1, s32[4,128]{1,0:T(4,128)} %bitcast.10, s32[4,128]{1,0:T(4,128)} %bitcast.11, s32[4]{0:T(128)} %wc_ref.1, f32[36,128]{1,0:T(8,128)} %bitcast.9, bf16[4096,128]{1,0:T(8,128)(2,1)} %bitcast.8, bf16[256,4608]{1,0:T(8,128)(2,1)} %ow_hbm.1, ...), custom_call_target="tpu_custom_call" | custom-call | tf_op jit(solution)/shard_map/layer/pallas_call | solution.py:456
  90.5 1.3 %copy.13 = bf16[2,4608]{1,0:T(2,128)(2,1)} copy(bf16[2,4608]{1,0:T(2,128)(2,1)} %layer.1) | data formatting | bytes 36864

commit v4 on v3

--- a/solution.py
+++ b/solution.py
@@ -35,12 +35,12 @@
 
 
 def kernel(
-    hid_ref, q_ref, kvm_ref, len_ref, wc_ref, gain_ref, kv_hbm, ow_hbm, wg_hbm, wu_hbm, wd_hbm,
+    hid_hbm, q_hbm, kvm_hbm, len_hbm, wc_hbm, gain_hbm, kv_hbm, ow_hbm, wg_hbm, wu_hbm, wd_hbm,
     out_ref,
-    kv_v, ow_v, wgu_v, wd_v,
-    qb, oh, oht, qs, ls, ns, nb, nr, nrx, sb, rb, g, xs, acc, ssq, hs, p, rx1, t, rx2, zb, rx3, res, gain, kvt, vs,
+    hid_ref, kvm_ref, len_ref, wc_ref, gain_ref, kv_v, ow_v, wgu_v, wd_v,
+    qb, oh, oht, qs, ls, ns, nb, nr, nrx, sb, rb, g, xs, acc, ssq, hs, p, rl, rx1, t, rx2, zb, rx3, res, gain, kvt, vs,
     lsem, a1s, a1r, a3s, a3r, bs, br, c1s, c1r, c2s, c2r, c3s, c3r,
-    wxs, wxr, d1s, d1r, d2s, d2r, d3s, d3r,
+    wxs, wxr, d0s, d0r, d1s, d1r, d2s, d2r, d3s, d3r,
 ):
     seq = lax.axis_index("seq")
     tp = lax.axis_index("tp")
@@ -49,7 +49,7 @@
     z = zh * 4 + zl
     sib = dev(x, y, z, 1 - c)
 
-    seq_offs = [(dy, dh) for dy in range(4) for dh in range(2) if (dy, dh) != (0, 0)]
+    seq_offs = [(2, 1), (1, 1), (3, 1), (0, 1), (2, 0), (1, 0), (3, 0)]
     tp_offs = [(dx, dl) for dx in (2, 1, 3, 0) for dl in (2, 1, 3, 0) if (dx, dl) != (0, 0)]
     peers = [sib]
     peers += [dev(x, (y + dy) % 4, ((zh + dh) % 2) * 4 + zl, c) for dy, dh in seq_offs]
@@ -66,21 +66,30 @@
         pltpu.make_async_copy(wu_hbm, wgu_v.at[1, c], lsem.at[3]),
         pltpu.make_async_copy(wd_hbm, wd_v.at[c], lsem.at[4]),
     ]
-    for load in loads:
+    small = [
+        pltpu.make_async_copy(q_hbm, qb.at[seq], lsem.at[5]),
+        pltpu.make_async_copy(kvm_hbm, kvm_ref, lsem.at[6]),
+        pltpu.make_async_copy(len_hbm, len_ref, lsem.at[7]),
+        pltpu.make_async_copy(gain_hbm, gain_ref, lsem.at[8]),
+        pltpu.make_async_copy(hid_hbm, hid_ref, lsem.at[9]),
+        pltpu.make_async_copy(wc_hbm, wc_ref, lsem.at[10]),
+    ]
+    for load in small + loads:
         load.start()
+    for load in small:
+        load.wait()
     pl.semaphore_wait(bar, len(peers))
 
     sends = []
     a1 = []
     for i, (dy, dh) in enumerate(seq_offs):
         to = dev(x, (y + dy) % 4, ((zh + dh) % 2) * 4 + zl, c)
-        cp = remote(q_ref, qb.at[seq], a1s.at[i], a1r.at[i], to)
+        cp = remote(qb.at[seq], qb.at[seq], a1s.at[i], a1r.at[i], to)
         cp.start()
         sends.append(cp)
-    cp = remote(q_ref, qb.at[seq], a1s.at[7], a1r.at[7], sib)
+    cp = remote(qb.at[seq], qb.at[seq], a1s.at[7], a1r.at[7], sib)
     cp.start()
     sends.append(cp)
-    qb[seq] = q_ref[...]
 
     row_id = lax.broadcasted_iota(jnp.int32, (512, 128), 0).astype(F32)
     lane_id = lax.broadcasted_iota(jnp.int32, (128, 128), 1).astype(F32)
@@ -111,14 +120,14 @@
         return 0
 
     lax.fori_loop(0, 16, prepare, 0)
-    for i, (dy, dh) in enumerate(seq_offs):
+    for i, (dy, dh) in reversed(list(enumerate(seq_offs))):
         frm = ((y - dy) % 4) * 4 + ((zh + dh) % 2) * 2 + c
-        a = remote(q_ref, qb.at[frm], a1s.at[i], a1r.at[i], sib)
+        a = remote(qb.at[seq], qb.at[frm], a1s.at[i], a1r.at[i], sib)
         a.wait_recv()
         cp = remote(qb.at[frm], qb.at[frm], a1s.at[8 + i], a1r.at[8 + i], sib)
         cp.start()
         sends.append(cp)
-    remote(q_ref, qb.at[seq], a1s.at[7], a1r.at[7], sib).wait_recv()
+    remote(qb.at[seq], qb.at[seq], a1s.at[7], a1r.at[7], sib).wait_recv()
     for i, (dy, dh) in enumerate(seq_offs):
         frm = ((y - dy) % 4) * 4 + ((zh + dh) % 2) * 2 + (1 - c)
         remote(qb.at[frm], qb.at[frm], a1s.at[8 + i], a1r.at[8 + i], sib).wait_recv()
@@ -184,23 +193,23 @@
         hi = both.astype(BF16).astype(F32)
         return both, jnp.where(low_half, hi, both - hi).astype(BF16)
 
-    def pair_sum(k, _):
+    def pair_sum(k):
         v = nb[c, k].astype(F32) + nr[k].astype(F32)
         nb[c, k, :, pl.ds(0, 256)] = v[:, :256].astype(BF16)
         nb[c, k, :, pl.ds(256, 128)] = split_total(v[:, 256:])[1]
-        return 0
-
-    lax.fori_loop(0, 8, pair_sum, 0)
+
     a3 = []
     for i, (dy, dh) in enumerate(seq_offs):
         yt, ht = (y + dy) % 4, (zh + dh) % 2
+        pair_sum(yt * 2 + ht)
         cp = remote(nb.at[c, yt * 2 + ht], nrx.at[i], a3s.at[i], a3r.at[i], dev(x, yt, ht * 4 + zl, c))
         cp.start()
         sends.append(cp)
         a3.append(cp)
+    pair_sum(y * 2 + zh)
     weights[1].start()
     total = nb[c, y * 2 + zh].astype(F32)
-    for i in range(7):
+    for i in reversed(range(7)):
         a3[i].wait_recv()
         total = total + nrx[i].astype(F32)
     tot = split_total(total[:, 256:])[0]
@@ -256,29 +265,37 @@
         load.wait()
     for weight in weights:
         weight.wait_recv()
-    for k in (1, 7, 2, 6, 3, 5, 4):
-        frm = (z + 8 - k) % 8
-        fh = frm // 4
-        piece = g.at[fh, x * (1 - fh) + y * fh, y * (1 - fh) + x * fh, frm % 4]
-        remote(piece, piece, c1s.at[k - 1], c1r.at[k - 1], sib).wait_recv()
-    for k in (1, 3, 2):
-        for h in range(2):
-            run = g.at[h, outer[h], inner[h]]
-            push(run, run, c2s.at[h, k - 1], c2r.at[h, k - 1], step(h, False, k))
-    for k in (1, 3, 2):
-        for h in range(2):
-            run = g.at[h, outer[h], inner[h]]
-            push(run, run, c3s.at[h, 0, k - 1], c3r.at[h, 0, k - 1], step(h, True, k))
+    for half, blocks in ((zh, [(zl + d) % 4 for d in (1, 3, 2)]), (1 - zh, range(4))):
+        ho, hi_ = x * (1 - half) + y * half, y * (1 - half) + x * half
+        for m in blocks:
+            k = (z + 7 - half * 4 - m) % 8
+            piece = g.at[half, ho, hi_, m]
+            remote(piece, piece, c1s.at[k], c1r.at[k], sib).wait_recv()
+        run = g.at[half, ho, hi_]
+        for k in (1, 3, 2):
+            to = dev((x + k * half) % 4, (y + k * (1 - half)) % 4, z, c)
+            push(run, run, c2s.at[half, k - 1], c2r.at[half, k - 1], to)
+        for k in (1, 3):
+            to = dev((x + k * (1 - half)) % 4, (y + k * half) % 4, z, c)
+            push(run, run, c3s.at[half, 0, k - 1], c3r.at[half, 0, k - 1], to)
+
+    def arrived(h, j, k):
+        run = g.at[h, (outer[h] + 4 - k) % 4, (inner[h] + 4 - j) % 4]
+        remote(run, run, c3s.at[h, j, k - 1], c3r.at[h, j, k - 1], sib).wait_recv()
+        return run
+
+    def relay(j, k):
+        for h in range(2):
+            run = arrived(h, j, k)
+            push(run, run, c3s.at[h, j, 1], c3r.at[h, j, 1], step(h, True, k))
+
     for j in (1, 3, 2):
         for h in range(2):
             run = g.at[h, outer[h], (inner[h] + 4 - j) % 4]
             remote(run, run, c2s.at[h, j - 1], c2r.at[h, j - 1], sib).wait_recv()
             for k in (1, 3):
                 push(run, run, c3s.at[h, j, k - 1], c3r.at[h, j, k - 1], step(h, True, k))
-    for j in (1, 3, 2):
-        for h in range(2):
-            run = g.at[h, outer[h], (inner[h] + 4 - j) % 4]
-            push(run, run, c3s.at[h, j, 1], c3r.at[h, j, 1], step(h, True, 2))
+    relay(0, 1)
 
     def partial(h, f, xq):
         cols = pl.ds(pl.multiple_of(xq * QD, 128), QD)
@@ -294,12 +311,17 @@
         squares(0, g[0, xq])
 
     first_half(x)
+    relay(3, 3)
+    relay(1, 1)
+    relay(2, 3)
+    rest = {1: (3, 2), 3: (0, 1), 2: (0, 3, 1, 2)}
     for k in (1, 3, 2):
-        for h in range(2):
-            for j in (0, 1, 3, 2):
-                run = g.at[h, (outer[h] + 4 - k) % 4, (inner[h] + 4 - j) % 4]
-                remote(run, run, c3s.at[h, j, k - 1], c3r.at[h, j, k - 1], sib).wait_recv()
+        for j in rest[k]:
+            arrived(0, j, k)
         first_half((x + 4 - k) % 4)
+    for k in (1, 3, 2):
+        for j in rest[k]:
+            arrived(1, j, k)
 
     def second_half(xq, _):
         partial(1, g[1, :, xq], xq)
@@ -323,10 +345,20 @@
         act = 0.5 * gate * (1.0 + jnp.tanh(0.7978845608028654 * (gate + 0.044715 * gate * gate * gate)))
         hs[pl.ds(h * 128, 128), :] = jnp.where(active, act * up, 0.0).astype(BF16)
 
-    def d1(k, h, off):
+    def along(k):
+        return jnp.where(k < 2, 0, 1)
+
+    def d0(k, h):
         return remote(
-            p.at[k, h, (outer[h] + off) % 4], rx1.at[k, h, off - 1],
-            d1s.at[k, h, off - 1], d1r.at[k, h, off - 1], step(h, True, off),
+            p.at[k, h, (outer[h] + 2) % 4], rl.at[k, h], d0s.at[k, h], d0r.at[k, h],
+            step(h, True, 1 + 2 * along(k)),
+        )
+
+    def d1(k, h, way):
+        off = 1 + 2 * way
+        return remote(
+            p.at[k, h, (outer[h] + off) % 4], rx1.at[k, h, way],
+            d1s.at[k, h, way], d1r.at[k, h, way], step(h, True, off),
         )
 
     def d2(k, h, off):
@@ -335,19 +367,31 @@
             d2s.at[k, h, off - 1], d2r.at[k, h, off - 1], step(h, False, off),
         )
 
-    def produce(k, _):
+    def produce(i, _):
+        k = (i % 2) * 2 + i // 2
         cols = pl.ds(pl.multiple_of(k * QD, 128), QD)
         v = jnp.dot(hs[...], wd_v[:, :, cols].reshape(2 * UNITS, QD), preferred_element_type=F32)
         v = v.astype(BF16).reshape(2, 4, 4, 8, QD)
         for w in range(4):
             p[k, 0, w] = v[0, :, w]
         p[k, 1] = v[1]
-        for off in (2, 1, 3):
-            for h in range(2):
-                d1(k, h, off).start()
+        for h in range(2):
+            d0(k, h).start()
+            d1(k, h, 1 - along(k)).start()
         return 0
 
     lax.fori_loop(0, 4, produce, 0)
+
+    def combine(i, _):
+        k = (i % 2) * 2 + i // 2
+        for h in range(2):
+            d0(k, h).wait_recv()
+            at = (outer[h] + 1 + 2 * along(k)) % 4
+            p[k, h, at] = (p[k, h, at].astype(F32) + rl[k, h].astype(F32)).astype(BF16)
+            d1(k, h, along(k)).start()
+        return 0
+
+    lax.fori_loop(0, 4, combine, 0)
 
     rid8 = lax.broadcasted_iota(jnp.int32, (8, QD), 0)
 
@@ -360,12 +404,13 @@
 
     lax.fori_loop(0, 4, own_rows, 0)
 
-    def outer_sum(k, _):
-        for h in range(2):
-            for off in (1, 3, 2):
-                d1(k, h, off).wait_recv()
+    def outer_sum(i, _):
+        k = (i % 2) * 2 + i // 2
+        for h in range(2):
+            for way in range(2):
+                d1(k, h, way).wait_recv()
             v = p[k, h, outer[h]].astype(F32)
-            for j in range(3):
+            for j in range(2):
                 v = v + rx1[k, h, j].astype(F32)
             t[k, h] = v.astype(BF16)
             for off in (2, 1, 3):
@@ -405,8 +450,10 @@
 
     def drain(k, _):
         for h in range(2):
+            d0(k, h).wait_send()
+            for way in range(2):
+                d1(k, h, way).wait_send()
             for off in (1, 2, 3):
-                d1(k, h, off).wait_send()
                 d2(k, h, off).wait_send()
         return 0
 
@@ -421,6 +468,8 @@
     hbm = pl.BlockSpec(memory_space=pl.ANY)
     V, S = pltpu.VMEM, pltpu.SemaphoreType.DMA
     scratch = [
+        V((2, D), BF16), V((4, 128), jnp.int32), V((4, 128), jnp.int32), pltpu.SMEM((4,), jnp.int32),
+        V((36, 128), F32),
         V((4096, 128), BF16), V((256, D), BF16), V((2, 2, UNITS, D), BF16), V((2, UNITS, D), BF16),
         V((16, 32, 256), BF16),
         V((512, 512), BF16),
@@ -439,7 +488,8 @@
         V((2, 128, 1), F32),
         V((256, 2 * UNITS), BF16),
         V((4, 2, 4, 4, 8, QD), BF16),
-        V((4, 2, 3, 4, 8, QD), BF16),
+        V((4, 2, 4, 8, QD), BF16),
+        V((4, 2, 2, 4, 8, QD), BF16),
         V((4, 2, 4, 8, QD), BF16),
         V((4, 2, 3, 8, QD), BF16),
         V((8, 2, D), BF16),
@@ -448,15 +498,15 @@
         V((1, D), F32),
         V((128, 4096), BF16),
         V((4096, 256), BF16),
-        S((5,)),
+        S((11,)),
         S((15,)), S((15,)), S((8,)), S((8,)), S((15,)), S((15,)),
         S((7,)), S((7,)), S((2, 3)), S((2, 3)), S((2, 4, 3)), S((2, 4, 3)),
-        S((3,)), S((3,)), S((4, 2, 3)), S((4, 2, 3)), S((4, 2, 3)), S((4, 2, 3)), S((7,)), S((7,)),
+        S((3,)), S((3,)), S((4, 2)), S((4, 2)), S((4, 2, 2)), S((4, 2, 2)), S((4, 2, 3)), S((4, 2, 3)), S((7,)), S((7,)),
     ]
     return pl.pallas_call(
         kernel,
         out_shape=jax.ShapeDtypeStruct((2, D), BF16),
-        in_specs=[vmem, vmem, vmem, vmem, pl.BlockSpec(memory_space=pltpu.SMEM), vmem] + [hbm] * 5,
+        in_specs=[hbm] * 11,
         out_specs=vmem,
         scratch_shapes=scratch,
         compiler_params=pltpu.CompilerParams(

time: 92.4 us -> 86.4 us (0.935)
  Pallas kernels: 90.5 us -> 84.9 us
    pallas_call x1, Pallas kernels: 90.5 us -> 84.9 us  [body(): pl.pallas_call(kernel, out_shape=jax.ShapeDtypeStruct((2, D), BF16), in_s...]
where the time goes in v4:
time: 86.4 us; the launch traced here: 86.3 us
  Pallas kernels  84.9 us (98%)
  local copies, waits for them, and re-layouts  1.34 us (2%)
    pallas_call x1, Pallas kernels, body(): pl.pallas_call(kernel, out_shape=jax.ShapeDtypeStruct((2, D), BF16), in_s...  84.9 us

profile of v4, /device:TPU:8, one launch (start us, length us, event | category | flops | bytes accessed | tf_op | source)
XLA Modules:
  0.0 86.3 jit_solution(4394361551384607405)
XLA Ops:
  0.0 84.9 %layer.1 = bf16[2,4608]{1,0:T(2,128)(2,1)} custom-call(bf16[2,4608]{1,0:T(2,128)(2,1)} %hid_hbm.1, bf16[32,256]{1,0:T(8,128)(2,1)} %q_hbm.1, s32[4,128]{1,0:T(4,128)} %bitcast.10, s32[4,128]{1,0:T(4,128)} %bitcast.11, s32[4]{0:T(128)} %wc_hbm.1, f32[36,128]{1,0:T(8,128)} %bitcast.9, bf16[4096,128]{1,0:T(8,128)(2,1)} %bitcast.8, bf16[256,4608]{1,0:T(8,128)(2,1)} %ow_hbm.1, ...), custom_call_target="tpu_custom_call" | custom-call | tf_op jit(solution)/shard_map/layer/pallas_call | solution.py:506
  84.9 1.3 %copy.13 = bf16[2,4608]{1,0:T(2,128)(2,1)} copy(bf16[2,4608]{1,0:T(2,128)(2,1)} %layer.1) | data formatting | bytes 36864

commit v5 on v4

--- a/solution.py
+++ b/solution.py
@@ -138,7 +138,6 @@
         remote(wd_hbm, wd_v.at[c], wxs.at[2], wxr.at[2], sib),
     ]
     sends += weights
-    weights[0].start()
     qs[...] = jnp.dot(
         oh[...], qb[...].reshape(512, 256), preferred_element_type=F32
     ).astype(BF16)
@@ -171,7 +170,7 @@
         ns[rows, pl.ds(256, 128)] = jnp.where(lane < 64, hi, both - hi).astype(BF16)
         return 0
 
-    lax.fori_loop(0, 16, attend, 0, unroll=4)
+    lax.fori_loop(0, 16, attend, 0, unroll=8)
 
     for k in range(4):
         v = jnp.dot(
@@ -207,6 +206,7 @@
         sends.append(cp)
         a3.append(cp)
     pair_sum(y * 2 + zh)
+    weights[0].start()
     weights[1].start()
     total = nb[c, y * 2 + zh].astype(F32)
     for i in reversed(range(7)):
@@ -272,7 +272,7 @@
             piece = g.at[half, ho, hi_, m]
             remote(piece, piece, c1s.at[k], c1r.at[k], sib).wait_recv()
         run = g.at[half, ho, hi_]
-        for k in (1, 3, 2):
+        for k in (2, 1, 3):
             to = dev((x + k * half) % 4, (y + k * (1 - half)) % 4, z, c)
             push(run, run, c2s.at[half, k - 1], c2r.at[half, k - 1], to)
         for k in (1, 3):
@@ -310,9 +310,9 @@
         partial(0, g[0, xq], xq)
         squares(0, g[0, xq])
 
-    first_half(x)
     relay(3, 3)
     relay(1, 1)
+    first_half(x)
     relay(2, 3)
     rest = {1: (3, 2), 3: (0, 1), 2: (0, 3, 1, 2)}
     for k in (1, 3, 2):

time: 86.4 us -> 85.9 us (level)
  no operation moved by 1% of the time
where the time goes in v5:
time: 85.9 us; the launch traced here: 85.7 us
  Pallas kernels  84.4 us (98%)
  local copies, waits for them, and re-layouts  1.34 us (2%)
    pallas_call x1, Pallas kernels, body(): pl.pallas_call(kernel, out_shape=jax.ShapeDtypeStruct((2, D), BF16), in_s...  84.4 us

profile of v5, /device:TPU:8, one launch (start us, length us, event | category | flops | bytes accessed | tf_op | source)
XLA Modules:
  0.0 85.7 jit_solution(3263006906058366454)
XLA Ops:
  0.0 84.4 %layer.1 = bf16[2,4608]{1,0:T(2,128)(2,1)} custom-call(bf16[2,4608]{1,0:T(2,128)(2,1)} %hid_hbm.1, bf16[32,256]{1,0:T(8,128)(2,1)} %q_hbm.1, s32[4,128]{1,0:T(4,128)} %bitcast.10, s32[4,128]{1,0:T(4,128)} %bitcast.11, s32[4]{0:T(128)} %wc_hbm.1, f32[36,128]{1,0:T(8,128)} %bitcast.9, bf16[4096,128]{1,0:T(8,128)(2,1)} %bitcast.8, bf16[256,4608]{1,0:T(8,128)(2,1)} %ow_hbm.1, ...), custom_call_target="tpu_custom_call" | custom-call | tf_op jit(solution)/shard_map/layer/pallas_call | solution.py:506
  84.4 1.3 %copy.13 = bf16[2,4608]{1,0:T(2,128)(2,1)} copy(bf16[2,4608]{1,0:T(2,128)(2,1)} %layer.1) | data formatting | bytes 36864

commit v6 on v5

--- a/solution.py
+++ b/solution.py
@@ -377,10 +377,17 @@
         p[k, 1] = v[1]
         for h in range(2):
             d0(k, h).start()
+        return 0
+
+    lax.fori_loop(0, 4, produce, 0)
+
+    def direct(i, _):
+        k = (i % 2) * 2 + i // 2
+        for h in range(2):
             d1(k, h, 1 - along(k)).start()
         return 0
 
-    lax.fori_loop(0, 4, produce, 0)
+    lax.fori_loop(0, 4, direct, 0)
 
     def combine(i, _):
         k = (i % 2) * 2 + i // 2

time: 85.9 us -> 85 us (0.990)
  Pallas kernels: 84.4 us -> 83.3 us
    pallas_call x1, Pallas kernels: 84.4 us -> 83.3 us  [body(): pl.pallas_call(kernel, out_shape=jax.ShapeDtypeStruct((2, D), BF16), in_s...]
where the time goes in v6:
time: 85 us; the launch traced here: 84.7 us
  Pallas kernels  83.3 us (98%)
  local copies, waits for them, and re-layouts  1.34 us (2%)
    pallas_call x1, Pallas kernels, body(): pl.pallas_call(kernel, out_shape=jax.ShapeDtypeStruct((2, D), BF16), in_s...  83.3 us

profile of v6, /device:TPU:8, one launch (start us, length us, event | category | flops | bytes accessed | tf_op | source)
XLA Modules:
  0.0 84.7 jit_solution(10027836161875965656)
XLA Ops:
  0.0 83.3 %layer.1 = bf16[2,4608]{1,0:T(2,128)(2,1)} custom-call(bf16[2,4608]{1,0:T(2,128)(2,1)} %hid_hbm.1, bf16[32,256]{1,0:T(8,128)(2,1)} %q_hbm.1, s32[4,128]{1,0:T(4,128)} %bitcast.10, s32[4,128]{1,0:T(4,128)} %bitcast.11, s32[4]{0:T(128)} %wc_hbm.1, f32[36,128]{1,0:T(8,128)} %bitcast.9, bf16[4096,128]{1,0:T(8,128)(2,1)} %bitcast.8, bf16[256,4608]{1,0:T(8,128)(2,1)} %ow_hbm.1, ...), custom_call_target="tpu_custom_call" | custom-call | tf_op jit(solution)/shard_map/layer/pallas_call | solution.py:513
  83.3 1.3 %copy.13 = bf16[2,4608]{1,0:T(2,128)(2,1)} copy(bf16[2,4608]{1,0:T(2,128)(2,1)} %layer.1) | data formatting | bytes 36864
